TPU v7x, 128 devices: a whole 4x4x4 slice. The times are simulated.
128 devices in a mesh: path: 32 (over z, x, core), shard: 4 (over y).
Axes of the slice: x: 4, y: 4, z: 4, core: 2. Of those that a mesh axis runs over, the one named last changes fastest.
Arguments:
- inputs: bfloat16 [65536, 2048], P('path', 'shard'), may hold values from -6 to 6
- out_grad: bfloat16 [65536, 2048], P('path', 'shard'), may hold values from -6 to 6
- path_weights: bfloat16 [32, 2048, 2048], P('path', 'shard'), may hold values from -6 to 6
- inner_drift: float32 [32, 2048, 2048], P('path', 'shard'), may hold values from -4 to 4
- path_module: int32 [32, 1], replicated, may hold values from 0 to 15
- module_slot: int32 [16], replicated, may hold values from 0 to 15, each once
- master: float32 [16, 2048, 2048], P(None, ('shard', 'path')), may hold values from -6 to 6
- momentum: float32 [16, 2048, 2048], P(None, ('shard', 'path')), may hold values from -4 to 4
Outputs:
- input_grad: bfloat16 [65536, 2048], P('path', 'shard')
- new_master: float32 [16, 2048, 2048], P(None, ('shard', 'path'))
- new_momentum: float32 [16, 2048, 2048], P(None, ('shard', 'path'))
- new_weights: bfloat16 [32, 2048, 2048], P('path', 'shard')
Inputs may be any that keep to these rules, and one draw needn't show every extreme that they name: `path_module`: every module is used by at least one path. `module_slot`: each slot holds exactly one module.
All inputs are finite; a program needn't handle non-finite values.
Results may differ from a plain program's by a relative error of at most 0.001.
Values may be sent and summed in bfloat16 or wider, within the bound.
No kernel may reach another device: no remote copies, remote signals or barrier semaphores. Data moves between devices by JAX's collectives and lax.ppermute only.
A program may use at most 192 MiB of HBM per device.

v0:
```python
import math

import jax
import jax.numpy as jnp
from jax import lax
from jax.sharding import PartitionSpec as P

inner_rate = 0.5
outer_rate = 0.7
momentum_coef = 0.9


def on_device(
    inputs, out_grad, path_weights, inner_drift, path_module, module_slot, master, momentum
):
    path_count = lax.axis_size("path")
    model_width = path_weights.shape[2]
    unit_scale = 1.0 / math.sqrt(model_width)
    weight_rows = path_weights[0]
    gathered = lax.all_gather(out_grad, "shard", axis=1, tiled=True)
    grad_raw = lax.dot_general(
        inputs, gathered, (((0,), (0,)), ((), ())), preferred_element_type=jnp.float32
    )
    back_raw = lax.dot_general(
        gathered, weight_rows, (((1,), (1,)), ((), ())), preferred_element_type=jnp.float32
    )
    pseudo = inner_drift[0] + inner_rate * (grad_raw * unit_scale)
    input_grad = (back_raw * unit_scale).astype(jnp.bfloat16)
    store_rows = master.shape[1]
    slot_total = master.shape[0]
    pieces = pseudo.reshape(path_count, store_rows, model_width)
    chosen = path_module[:, 0]
    matches = chosen[:, None] == jnp.arange(module_slot.shape[0], dtype=jnp.int32)[None, :]
    slot_of_path = jnp.sum(jnp.where(matches, module_slot[None, :], 0), axis=1)
    member = (slot_of_path[None, :] == jnp.arange(slot_total, dtype=jnp.int32)[:, None]).astype(
        jnp.float32
    )
    counts = jnp.sum(member, axis=1)
    received = lax.all_to_all(pieces, "path", split_axis=0, concat_axis=0, tiled=True)
    row_count = received.shape[1]
    flattened = received.reshape(path_count, row_count * model_width)
    summed = jnp.dot(member, flattened, precision=lax.Precision.HIGHEST)
    slot_sums = summed.reshape(slot_total, row_count, model_width)
    slot_mean = slot_sums / counts[:, None, None]
    new_momentum = momentum_coef * momentum + slot_mean
    new_master = master - outer_rate * (slot_mean + momentum_coef * new_momentum)
    whole_store = lax.all_gather(new_master.astype(jnp.bfloat16), "path", axis=1, tiled=True)
    own_slot = jnp.sum(
        jnp.where(
            jnp.arange(path_count, dtype=jnp.int32) == lax.axis_index("path"), slot_of_path, 0
        )
    )
    new_weights = lax.dynamic_slice_in_dim(whole_store, own_slot, 1, 0)
    return (input_grad, new_master, new_momentum, new_weights)


def solution(mesh):
    placed = (
        P("path", "shard"),
        P("path", "shard"),
        P("path", "shard", None),
        P("path", "shard", None),
        P(),
        P(),
        P(None, ("shard", "path"), None),
        P(None, ("shard", "path"), None),
    )
    return jax.shard_map(
        on_device,
        mesh=mesh,
        in_specs=placed,
        out_specs=(
            P("path", "shard"),
            P(None, ("shard", "path"), None),
            P(None, ("shard", "path"), None),
            P("path", "shard", None),
        ),
        check_vma=False,
    )
```

profile of v0, /device:TPU:0, one launch (start us, length us, event | category | flops | bytes accessed | tf_op | source)
XLA Modules:
  0.0 305.3 jit_solution(79702532055584036)
XLA Ops:
  7.2 0.0 copy-start
  7.2 0.0 all-gather.3.cloned.1.call-start
  7.2 0.7 all-gather.3.cloned.1.call-update
  7.9 87.4 %all-gather.3.cloned.1.call-done = bf16[2048,2048]{1,0:T(8,128)(2,1)} async-done(((bf16[2048,512]{1,0:T(8,128)(2,1)}), bf16[2048,2048]{1,0:T(8,128)(2,1)}) %all-gather.3.cloned.1.call-update) | async-done | bytes 8388624 | tf_op jit(solution)/shard_map/all_gather | solution.py:20
  95.3 0.0 copy-done
  95.3 10.1 %bitcast_add_fusion = f32[512,2048]{1,0:T(8,128)} fusion(f32[1,512,2048]{2,1,0:T(8,128)} %param.11, bf16[2048,512]{1,0:T(8,128)(2,1)S(1)} %copy-done, bf16[2048,2048]{1,0:T(8,128)(2,1)} %all-gather.3.cloned.1.call-done), kind=kOutput, calls=%fused_computation.3 | convolution fusion | flops 4297064448 | bytes 18874368 | tf_op jit(solution)/shard_map/dot_general | solution.py:21
  105.4 0.0 copy-start.3
  105.4 0.0 copy-start.4
  105.4 7.5 %all-to-all-start = ((f32[32,16,2048]{2,1,0:T(8,128)}), f32[32,16,2048]{2,1,0:T(8,128)}, u32[]{:S(2)}, u32[]{:S(2)}) async-start(f32[32,16,2048]{2,1,0:T(8,128)} %bitcast.30), calls=%async_computation | async-start | bytes 8388608 | tf_op jit(solution)/shard_map/all_to_all | solution.py:39
  112.9 0.2 all-gather.5.cloned.1.call-start
  113.2 0.0 copy-done.3
  113.2 0.0 copy-done.4
  113.2 0.1 select_reduce_fusion
  113.3 0.1 convert_reduce_fusion
  113.4 53.0 %all-to-all-done = f32[32,16,2048]{2,1,0:T(8,128)} async-done(((f32[32,16,2048]{2,1,0:T(8,128)}), f32[32,16,2048]{2,1,0:T(8,128)}, u32[]{:S(2)}, u32[]{:S(2)}) %all-to-all-start) | async-done | bytes 4194336 | tf_op jit(solution)/shard_map/all_to_all | solution.py:39
  166.4 11.3 %fusion.12 = (bf16[16,16,2048]{2,0,1:T(8,128)(2,1)}, f32[16,16,2048]{2,0,1:T(8,128)}, f32[16,16,2048]{2,0,1:T(8,128)S(1)}) fusion(f32[16,16,2048]{2,1,0:T(8,128)} %param.15, f32[16,16,2048]{2,1,0:T(8,128)} %param.14, f32[16]{0:T(128)S(1)} %convert_reduce_fusion, s32[32]{0:T(128)S(1)} %select_reduce_fusion, f32[4,8,16,2048]{3,2,1,0:T(8,128)} %bitcast.8), kind=kOutput, calls=%fused_computation.19 | convolution fusion | flops 205521408 | bytes 13631680 | tf_op jit(solution)/shard_map/dot_general | solution.py:42
  177.7 0.0 all-gather.5.cloned.1.call-update
  177.7 0.6 fusion.11
  180.3 0.0 copy-start.2
  180.3 10.3 %multiply_convert_fusion = bf16[2048,512]{1,0:T(8,128)(2,1)} fusion(bf16[2048,2048]{1,0:T(8,128)(2,1)} %all-gather.3.cloned.1.call-done, bf16[1,512,2048]{2,1,0:T(8,128)(2,1)} %param.10), kind=kOutput, calls=%fused_computation.4 | convolution fusion | flops 4297064448 | bytes 12582912 | tf_op jit(solution)/shard_map/dot_general | solution.py:24
  190.6 0.0 copy-done.2
  190.6 2.8 copy.32
  193.4 2.5 copy.33
  195.9 92.4 %all-gather.5.cloned.1.call-done = bf16[16,512,2048]{2,0,1:T(8,128)(2,1)} async-done(((bf16[16,16,2048]{2,0,1:T(8,128)(2,1)}), bf16[16,512,2048]{2,0,1:T(8,128)(2,1)}) %all-gather.5.cloned.1.call-update) | async-done | bytes 33554448 | tf_op jit(solution)/shard_map/all_gather | solution.py:47
  288.3 0.0 copy-start.1
  288.3 7.5 %constant_dynamic-slice_fusion = bf16[1,512,2048]{2,0,1:T(2,128)(2,1)S(1)} fusion(bf16[16,512,2048]{2,0,1:T(8,128)(2,1)} %all-gather.5.cloned.1.call-done, s32[]{:T(128)S(6)} %select_n.13), kind=kLoop, calls=%fused_computation.18 | loop fusion | bytes 4194308 | tf_op jit(solution)/shard_map/dynamic_slice | solution.py:53
  295.9 2.6 copy.34
  298.5 0.0 copy-done.1
Async XLA Ops:
  7.2 88.1 %copy-start = (bf16[2048,512]{1,0:T(8,128)(2,1)S(1)}, bf16[2048,512]{1,0:T(8,128)(2,1)}, u32[]{:S(2)}) copy-start(bf16[2048,512]{1,0:T(8,128)(2,1)} %param.8) | copy-start | bytes 6291460
  7.2 88.1 %all-gather.3.cloned.1.call-start = ((), (), s32[]{:S(2)}) async-start(), calls=%async_computation.1 | async-start | bytes 10485760 | tf_op jit(solution)/shard_map/all_gather | solution.py:20
  105.4 7.7 %copy-start.3 = (s32[16]{0:T(128)S(1)}, s32[16]{0:T(128)}, u32[]{:S(2)}) copy-start(s32[16]{0:T(128)} %param.13) | copy-start | bytes 196
  105.4 7.7 %copy-start.4 = (s32[32,1]{0,1:T(1,128)S(1)}, s32[32,1]{0,1:T(1,128)}, u32[]{:S(2)}) copy-start(s32[32,1]{0,1:T(1,128)} %param.12) | copy-start | bytes 388
  105.4 61.0 %all-to-all-start = ((f32[32,16,2048]{2,1,0:T(8,128)}), f32[32,16,2048]{2,1,0:T(8,128)}, u32[]{:S(2)}, u32[]{:S(2)}) async-start(f32[32,16,2048]{2,1,0:T(8,128)} %bitcast.30), calls=%async_computation | async-start | bytes 8388608 | tf_op jit(solution)/shard_map/all_to_all | solution.py:39
  112.9 175.4 %all-gather.5.cloned.1.call-start = ((), (), s32[]{:S(2)}) async-start(), calls=%async_computation.2 | async-start | bytes 34603008 | tf_op jit(solution)/shard_map/all_gather | solution.py:47
  180.3 10.4 %copy-start.2 = (f32[16,16,2048]{2,0,1:T(8,128)S(1)}, f32[16,16,2048]{2,0,1:T(8,128)}, u32[]{:S(2)}) copy-start(f32[16,16,2048]{2,0,1:T(8,128)} %get-tuple-element.21) | copy-start | bytes 6291460
  288.3 10.1 %copy-start.1 = (bf16[2048,512]{1,0:T(8,128)(2,1)S(1)}, bf16[2048,512]{1,0:T(8,128)(2,1)}, u32[]{:S(2)}) copy-start(bf16[2048,512]{1,0:T(8,128)(2,1)} %param.8) | copy-start | bytes 6291460
Sparse Core Ops, SparseCore 0:
  9.7 85.5 all-gather.2
  177.8 110.4 all-gather.4
where the time goes:
time: 307 us; the launch traced here: 305 us
  waiting for transfers between devices  233 us (76%)
  matrix products  31.7 us (10%)
  between operations  16 us (5%)
  local copies, waits for them, and re-layouts  15.5 us (5%)
  starting transfers between devices  7.75 us (3%)
    all_gather x1, waiting for transfers between devices, on_device(): lax.all_gather(new_master.astype(jnp.bfloat16), 'path', axis=1, tiled=True)  92.4 us
    all_gather x1, waiting for transfers between devices, on_device(): gathered = lax.all_gather(out_grad, 'shard', axis=1, tiled=True)  87.4 us
    all_to_all x1, waiting for transfers between devices, on_device(): lax.all_to_all(pieces, 'path', split_axis=0, concat_axis=0, tiled=True)  53 us
    dot_general x1, matrix products, on_device(): summed = jnp.dot(member, flattened, precision=lax.Precision.HIGHEST)  11.3 us
    dot_general x1, matrix products, on_device(): lax.dot_general(gathered, weight_rows, (((1,), (1,)), ((), ())), preferre...  10.3 us
    dot_general x1, matrix products, on_device(): lax.dot_general(inputs, gathered, (((0,), (0,)), ((), ())), preferred_ele...  10.1 us
    unnamed x13, local copies, waits for them, and re-layouts  7.91 us
    dynamic_slice x1, local copies, waits for them, and re-layouts, on_device(): new_weights = lax.dynamic_slice_in_dim(whole_store, own_slot, 1, 0)  7.54 us
  transfers between devices with their start and end apart: 3, of which 3 were waited for; matrix products, arithmetic and copies ran while one was open for 5% of the time, Pallas kernels for 0%

commit v1 on v0

v1 whole, which is shorter than its diff:
```python
import math

import jax
import jax.numpy as jnp
from jax import lax
from jax.sharding import PartitionSpec as P

inner_rate = 0.5
outer_rate = 0.7
momentum_coef = 0.9


def ring_gather(block):
    size = lax.axis_size("shard")
    up = [(i, (i + 1) % size) for i in range(size)]
    down = [(i, (i - 1) % size) for i in range(size)]
    half = block.shape[1] // 2
    left = lax.ppermute(block, "shard", up)
    right = lax.ppermute(block, "shard", down)
    far_a = lax.ppermute(left[:, :half], "shard", up)
    far_b = lax.ppermute(right[:, half:], "shard", down)
    return block, left, right, jnp.concatenate([far_a, far_b], axis=1)


def on_device(
    inputs, out_grad, path_weights, inner_drift, path_module, module_slot, master, momentum
):
    path_count = lax.axis_size("path")
    shards = lax.axis_size("shard")
    me = lax.axis_index("shard")
    model_width = path_weights.shape[2]
    width = out_grad.shape[1]
    unit_scale = 1.0 / math.sqrt(model_width)
    blocks = ring_gather(out_grad)
    owners = [me, (me + shards - 1) % shards, (me + 1) % shards, (me + 2) % shards]
    gathered = jnp.zeros((out_grad.shape[0], model_width), out_grad.dtype)
    for block, owner in zip(blocks, owners):
        gathered = lax.dynamic_update_slice(gathered, block, (0, owner * width))

    chosen = path_module[:, 0]
    matches = chosen[:, None] == jnp.arange(module_slot.shape[0], dtype=jnp.int32)[None, :]
    slot_of_path = jnp.sum(jnp.where(matches, module_slot[None, :], 0), axis=1)
    slot_total = master.shape[0]
    member = (slot_of_path[None, :] == jnp.arange(slot_total, dtype=jnp.int32)[:, None]).astype(
        jnp.float32
    )
    counts = jnp.sum(member, axis=1)

    grad_raw = lax.dot_general(
        inputs, gathered, (((0,), (0,)), ((), ())), preferred_element_type=jnp.float32
    )
    pseudo = inner_drift[0] + inner_rate * (grad_raw * unit_scale)
    store_rows = master.shape[1]
    pieces = pseudo.astype(jnp.float16).reshape(path_count, store_rows, model_width)
    received = lax.all_to_all(pieces, "path", split_axis=0, concat_axis=0, tiled=True)
    back_raw = lax.dot_general(
        gathered, path_weights[0], (((1,), (1,)), ((), ())), preferred_element_type=jnp.float32
    )
    input_grad = (back_raw * unit_scale).astype(jnp.bfloat16)

    flattened = received.astype(jnp.float32).reshape(path_count, store_rows * model_width)
    summed = jnp.dot(member, flattened, precision=lax.Precision.HIGHEST)
    slot_sums = summed.reshape(slot_total, store_rows, model_width)
    slot_mean = slot_sums / counts[:, None, None]
    new_momentum = momentum_coef * momentum + slot_mean
    new_master = master - outer_rate * (slot_mean + momentum_coef * new_momentum)
    rounded = new_master.astype(jnp.bfloat16)
    outgoing = jnp.take(rounded, slot_of_path, axis=0)
    back = lax.all_to_all(outgoing, "path", split_axis=0, concat_axis=0, tiled=True)
    new_weights = back.reshape(1, path_count * store_rows, model_width)
    return (input_grad, new_master, new_momentum, new_weights)


def solution(mesh):
    placed = (
        P("path", "shard"),
        P("path", "shard"),
        P("path", "shard", None),
        P("path", "shard", None),
        P(),
        P(),
        P(None, ("shard", "path"), None),
        P(None, ("shard", "path"), None),
    )
    return jax.shard_map(
        on_device,
        mesh=mesh,
        in_specs=placed,
        out_specs=(
            P("path", "shard"),
            P(None, ("shard", "path"), None),
            P(None, ("shard", "path"), None),
            P("path", "shard", None),
        ),
        check_vma=False,
    )
```

time: 307 us -> 180 us (0.59)
  waiting for transfers between devices: 233 us -> 106 us
  between operations: 16 us -> 0.77 us
  starting transfers between devices: 7.75 us -> 20 us
  matrix products: 31.7 us -> 26.4 us
  local copies, waits for them, and re-layouts: 15.5 us -> 20.6 us
  other arithmetic: 0.84 us -> 4.92 us
    all_gather x2 -> x0, waiting for transfers between devices: 180 us -> none  [the longest x1 92.4 us: on_device(): lax.all_gather(new_master.astype(jnp.bfloat16), 'path', axis=1, tiled=True)]
    ppermute x0 -> x4, waiting for transfers between devices: none -> 62.3 us  [the longest x1 45.7 us: ring_gather(): left = lax.ppermute(block, 'shard', up)]
    all_to_all x1, waiting for transfers between devices: 53 us -> 29.5 us  [on_device(): lax.all_to_all(pieces, 'path', split_axis=0, concat_axis=0, tiled=True)]
    all_to_all x0 -> x1, waiting for transfers between devices: none -> 14.6 us  [on_device(): lax.all_to_all(outgoing, 'path', split_axis=0, concat_axis=0, tiled=True)]
    dynamic_slice x1 -> x0, local copies, waits for them, and re-layouts: 7.54 us -> none  [on_device(): new_weights = lax.dynamic_slice_in_dim(whole_store, own_slot, 1, 0)]
    ppermute x0 -> x4, starting transfers between devices: none -> 6.54 us  [the longest x1 2.94 us: ring_gather(): far_b = lax.ppermute(right[:, half:], 'shard', down)]
    unnamed x13 -> x27, local copies, waits for them, and re-layouts: 7.91 us -> 13.9 us
    all_to_all x0 -> x1, starting transfers between devices: none -> 4.98 us  [on_device(): lax.all_to_all(outgoing, 'path', split_axis=0, concat_axis=0, tiled=True)]
  transfers between devices with their start and end apart: 3 -> 6, of which waited for: 3 -> 5; matrix products, arithmetic and copies ran while one was open for 5% -> 11% of each run, Pallas kernels for 0% -> 0%
where the time goes in v1:
time: 180 us; the launch traced here: 179 us
  waiting for transfers between devices  106 us (59%)
  matrix products  26.4 us (15%)
  local copies, waits for them, and re-layouts  20.6 us (11%)
  starting transfers between devices  20 us (11%)
  other arithmetic  4.92 us (3%)
    ppermute x1, waiting for transfers between devices, ring_gather(): left = lax.ppermute(block, 'shard', up)  45.7 us
    all_to_all x1, waiting for transfers between devices, on_device(): lax.all_to_all(pieces, 'path', split_axis=0, concat_axis=0, tiled=True)  29.5 us
    ppermute x1, waiting for transfers between devices, ring_gather(): far_a = lax.ppermute(left[:, :half], 'shard', up)  14.9 us
    all_to_all x1, waiting for transfers between devices, on_device(): lax.all_to_all(outgoing, 'path', split_axis=0, concat_axis=0, tiled=True)  14.6 us
    unnamed x27, local copies, waits for them, and re-layouts  13.9 us
    dot_general x1, matrix products, on_device(): summed = jnp.dot(member, flattened, precision=lax.Precision.HIGHEST)  10.5 us
    dot_general x1, matrix products, on_device(): lax.dot_general(gathered, path_weights[0], (((1,), (1,)), ((), ())), pref...  10 us
    all_to_all x1, starting transfers between devices, on_device(): lax.all_to_all(pieces, 'path', split_axis=0, concat_axis=0, tiled=True)  8.51 us
  transfers between devices with their start and end apart: 6, of which 5 were waited for; matrix products, arithmetic and copies ran while one was open for 11% of the time, Pallas kernels for 0%

profile of v1, /device:TPU:0, one launch (start us, length us, event | category | flops | bytes accessed | tf_op | source)
XLA Modules:
  0.0 179.3 jit_solution(14988952798420831268)
XLA Ops:
  0.6 0.0 copy-start
  0.6 1.7 collective-permute-start
  2.4 1.6 collective-permute-start.1
  4.0 45.7 %collective-permute-done = bf16[2048,512]{1,0:T(8,128)(2,1)S(1)} collective-permute-done((bf16[2048,512]{1,0:T(8,128)(2,1)}, bf16[2048,512]{1,0:T(8,128)(2,1)S(1)}, u32[]{:S(2)}, u32[]{:S(2)}) %collective-permute-start) | collective-permute-done | bytes 2097184 | tf_op jit(solution)/shard_map/ppermute | solution.py:18
  49.7 0.0 copy-start.2
  49.7 1.3 copy-done.2
  51.0 1.0 slice.10
  52.0 0.3 collective-permute-start.2
  52.3 0.0 collective-permute-done.1
  52.3 0.0 copy-start.4
  52.3 1.3 copy-done.4
  53.6 1.0 slice.11
  54.7 2.9 %collective-permute-start.3 = (bf16[2048,256]{1,0:T(8,128)(2,1)}, bf16[2048,256]{1,0:T(8,128)(2,1)}, u32[]{:S(2)}, u32[]{:S(2)}) collective-permute-start(bf16[2048,256]{1,0:T(8,128)(2,1)} %slice.11), channel_id=1, source_target_pairs={{0,3},{1,0},{2,1},{3,2},{4,7},{5,4},{6,5},{7,6},{8,11},{9,8},{10,9... | collective-permute-start | bytes 3145736 | tf_op jit(solution)/shard_map/ppermute | solution.py:21
  57.6 0.0 copy-start.6
  57.6 1.1 broadcast_in_dim.30
  58.7 0.5 copy-done.6
  59.2 0.0 copy-start.3
  59.2 0.3 constant_dynamic-update-slice_fusion.2
  59.5 1.2 copy-done.3
  60.8 0.0 copy-start.5
  60.8 0.3 constant_dynamic-update-slice_fusion.1
  61.1 1.2 copy-done.5
  62.4 0.3 constant_dynamic-update-slice_fusion
  62.7 0.0 copy-start.9
  62.7 14.9 %collective-permute-done.2 = bf16[2048,256]{1,0:T(8,128)(2,1)S(1)} collective-permute-done((bf16[2048,256]{1,0:T(8,128)(2,1)}, bf16[2048,256]{1,0:T(8,128)(2,1)S(1)}, u32[]{:S(2)}, u32[]{:S(2)}) %collective-permute-start.2) | collective-permute-done | bytes 1048608 | tf_op jit(solution)/shard_map/ppermute | solution.py:20
  77.6 1.7 collective-permute-done.3
  79.4 1.5 maximum_dynamic-update-slice_fusion
  80.9 0.0 copy-done
  80.9 0.0 copy-done.9
  80.9 0.0 copy-start.1
  80.9 5.9 %fusion = f16[512,2048]{1,0:T(8,128)(2,1)} fusion(f32[1,512,2048]{2,1,0:T(8,128)S(1)} %copy-done.9, bf16[2048,2048]{1,0:T(8,128)(2,1)S(1)} %maximum_dynamic-update-slice_fusion, bf16[2048,512]{1,0:T(8,128)(2,1)S(1)} %copy-done), kind=kOutput, calls=%fused_computation.2 | convolution fusion | flops 4298113024 | bytes 16777216 | tf_op jit(solution)/shard_map/dot_general | solution.py:49
  86.9 0.0 copy-done.1
  86.9 0.0 copy-start.10
  86.9 0.0 copy-start.11
  86.9 8.5 %all-to-all-start = ((f16[32,16,2048]{2,1,0:T(8,128)(2,1)}), f16[32,16,2048]{2,1,0:T(8,128)(2,1)}, u32[]{:S(2)}, u32[]{:S(2)}) async-start(f16[32,16,2048]{2,1,0:T(8,128)(2,1)} %bitcast.37), calls=%async_computation | async-start | bytes 4194304 | tf_op jit(solution)/shard_map/all_to_all | solution.py:55
  95.4 0.0 copy-done.10
  95.4 0.0 copy-done.11
  95.4 0.1 select_reduce_fusion
  95.5 0.1 convert_reduce_fusion
  95.6 29.5 %all-to-all-done = f16[32,16,2048]{2,1,0:T(8,128)(2,1)} async-done(((f16[32,16,2048]{2,1,0:T(8,128)(2,1)}), f16[32,16,2048]{2,1,0:T(8,128)(2,1)}, u32[]{:S(2)}, u32[]{:S(2)}) %all-to-all-start) | async-done | bytes 2097184 | tf_op jit(solution)/shard_map/all_to_all | solution.py:55
  125.2 10.5 %fusion.9 = (bf16[16,16,2048]{2,0,1:T(8,128)(2,1)S(1)}, f32[16,16,2048]{2,0,1:T(8,128)}, f32[16,16,2048]{2,0,1:T(8,128)}) fusion(f32[16,16,2048]{2,1,0:T(8,128)} %param.15, f32[16,16,2048]{2,1,0:T(8,128)} %param.14, f32[16]{0:T(128)S(1)} %convert_reduce_fusion, s32[32]{0:T(128)S(1)} %select_reduce_fusion, f16[4,8,16,2048]{3,2,1,0:T(8,128)(2,1)} %bitcast.12), kind=kOutput, calls=%fused_computation.27 | convolution fusion | flops 37749248 | bytes 11534528 | tf_op jit(solution)/shard_map/dot_general | solution.py:62
  135.7 0.6 copy.25
  136.2 2.0 %gather_fusion = bf16[32,16,2048]{2,1,0:T(8,128)(2,1)} fusion(bf16[16,16,2048]{2,1,0:T(8,128)(2,1)S(1)} %copy.25, s32[1024]{0:T(1024)S(1)} %pad_clamp_fusion), kind=kCustom, calls=%fused_computation | custom fusion | bytes 4194432 | tf_op jit(solution)/shard_map/jit(_take)/gather | solution.py:68
  138.2 3.2 %broadcast_select_fusion = bf16[32,16,2048]{2,1,0:T(8,128)(2,1)} fusion(bf16[32,16,2048]{2,1,0:T(8,128)(2,1)} %gather_fusion, pred[32]{0:T(512)(128)(4,1)S(1)} %compare_and_fusion), kind=kLoop, calls=%fused_computation.12 | loop fusion | flops 1048576 | bytes 4194336 | tf_op jit(solution)/shard_map/jit(_take)/select_n | solution.py:68
  141.4 5.0 %all-to-all-start.1 = ((bf16[32,16,2048]{2,1,0:T(8,128)(2,1)}), bf16[32,16,2048]{2,1,0:T(8,128)(2,1)}, u32[]{:S(2)}, u32[]{:S(2)}) async-start(bf16[32,16,2048]{2,1,0:T(8,128)(2,1)} %broadcast_select_fusion), calls=%async_computation.1 | async-start | bytes 4194304 | tf_op jit(solution)/shard_map/all_to_all | solution.py:69
  146.4 0.0 copy-start.8
  146.4 10.0 %multiply_convert_fusion = bf16[2048,512]{1,0:T(8,128)(2,1)} fusion(bf16[2048,2048]{1,0:T(8,128)(2,1)} %copy-done.1, bf16[1,512,2048]{2,1,0:T(8,128)(2,1)} %param.10), kind=kOutput, calls=%fused_computation.3 | convolution fusion | flops 4297064448 | bytes 12582912 | tf_op jit(solution)/shard_map/dot_general | solution.py:56
  156.4 0.0 copy-done.8
  156.4 0.0 copy-start.7
  156.4 2.5 %copy.26 = f32[16,16,2048]{2,1,0:T(8,128)} copy(f32[16,16,2048]{2,0,1:T(8,128)S(1)} %copy-done.8) | data formatting | bytes 4194304
  159.0 0.0 copy-done.7
  159.0 2.5 %copy.27 = f32[16,16,2048]{2,1,0:T(8,128)} copy(f32[16,16,2048]{2,0,1:T(8,128)S(1)} %copy-done.7) | data formatting | bytes 4194304
  161.5 14.6 %all-to-all-done.1 = bf16[32,16,2048]{2,1,0:T(8,128)(2,1)} async-done(((bf16[32,16,2048]{2,1,0:T(8,128)(2,1)}), bf16[32,16,2048]{2,1,0:T(8,128)(2,1)}, u32[]{:S(2)}, u32[]{:S(2)}) %all-to-all-start.1) | async-done | bytes 2097184 | tf_op jit(solution)/shard_map/all_to_all | solution.py:69
  176.1 3.2 %copy.52 = bf16[1,512,2048]{2,1,0:T(8,128)(2,1)} copy(bf16[1,512,2048]{2,1,0:T(8,128)(2,1)} %bitcast.9) | data formatting | bytes 4194304
  (3 shorter events, 0.0 us)
Async XLA Ops:
  0.6 80.3 %copy-start = (bf16[2048,512]{1,0:T(8,128)(2,1)S(1)}, bf16[2048,512]{1,0:T(8,128)(2,1)}, u32[]{:S(2)}) copy-start(bf16[2048,512]{1,0:T(8,128)(2,1)} %param.8) | copy-start | bytes 6291460
  0.6 49.0 %collective-permute-start = (bf16[2048,512]{1,0:T(8,128)(2,1)}, bf16[2048,512]{1,0:T(8,128)(2,1)S(1)}, u32[]{:S(2)}, u32[]{:S(2)}) collective-permute-start(bf16[2048,512]{1,0:T(8,128)(2,1)} %param.9), channel_id=1, source_target_pairs={{0,1},{1,2},{2,3},{3,0},{4,5},{5,6},{6,7},{7,4},{8,9},{9,10},{10,1... | collective-permute-start | bytes 6291464 | tf_op jit(solution)/shard_map/ppermute | solution.py:18
  2.4 49.9 %collective-permute-start.1 = (bf16[2048,512]{1,0:T(8,128)(2,1)}, bf16[2048,512]{1,0:T(8,128)(2,1)S(1)}, u32[]{:S(2)}, u32[]{:S(2)}) collective-permute-start(bf16[2048,512]{1,0:T(8,128)(2,1)} %param.9), channel_id=1, source_target_pairs={{0,3},{1,0},{2,1},{3,2},{4,7},{5,4},{6,5},{7,6},{8,11},{9,8},{10,9... | collective-permute-start | bytes 6291464 | tf_op jit(solution)/shard_map/ppermute | solution.py:19
  49.7 1.3 copy-start.2
  52.0 25.6 %collective-permute-start.2 = (bf16[2048,256]{1,0:T(8,128)(2,1)}, bf16[2048,256]{1,0:T(8,128)(2,1)S(1)}, u32[]{:S(2)}, u32[]{:S(2)}) collective-permute-start(bf16[2048,256]{1,0:T(8,128)(2,1)} %slice.10), channel_id=1, source_target_pairs={{0,1},{1,2},{2,3},{3,0},{4,5},{5,6},{6,7},{7,4},{8,9},{9,10},{10,1... | collective-permute-start | bytes 3145736 | tf_op jit(solution)/shard_map/ppermute | solution.py:20
  52.3 1.3 copy-start.4
  54.7 24.7 %collective-permute-start.3 = (bf16[2048,256]{1,0:T(8,128)(2,1)}, bf16[2048,256]{1,0:T(8,128)(2,1)}, u32[]{:S(2)}, u32[]{:S(2)}) collective-permute-start(bf16[2048,256]{1,0:T(8,128)(2,1)} %slice.11), channel_id=1, source_target_pairs={{0,3},{1,0},{2,1},{3,2},{4,7},{5,4},{6,5},{7,6},{8,11},{9,8},{10,9... | collective-permute-start | bytes 3145736 | tf_op jit(solution)/shard_map/ppermute | solution.py:21
  57.6 1.6 copy-start.6
  59.2 1.6 copy-start.3
  60.8 1.6 copy-start.5
  62.7 18.2 %copy-start.9 = (f32[1,512,2048]{2,1,0:T(8,128)S(1)}, f32[1,512,2048]{2,1,0:T(8,128)}, u32[]{:S(2)}) copy-start(f32[1,512,2048]{2,1,0:T(8,128)} %param.11) | copy-start | bytes 12582916
  80.9 5.9 %copy-start.1 = (bf16[2048,2048]{1,0:T(8,128)(2,1)}, bf16[2048,2048]{1,0:T(8,128)(2,1)S(1)}, u32[]{:S(2)}) copy-start(bf16[2048,2048]{1,0:T(8,128)(2,1)S(1)} %maximum_dynamic-update-slice_fusion) | copy-start | bytes 25165828
  86.9 8.5 %copy-start.10 = (s32[16]{0:T(128)S(1)}, s32[16]{0:T(128)}, u32[]{:S(2)}) copy-start(s32[16]{0:T(128)} %param.13) | copy-start | bytes 196
  86.9 8.5 %copy-start.11 = (s32[32,1]{0,1:T(1,128)S(1)}, s32[32,1]{0,1:T(1,128)}, u32[]{:S(2)}) copy-start(s32[32,1]{0,1:T(1,128)} %param.12) | copy-start | bytes 388
  86.9 38.3 %all-to-all-start = ((f16[32,16,2048]{2,1,0:T(8,128)(2,1)}), f16[32,16,2048]{2,1,0:T(8,128)(2,1)}, u32[]{:S(2)}, u32[]{:S(2)}) async-start(f16[32,16,2048]{2,1,0:T(8,128)(2,1)} %bitcast.37), calls=%async_computation | async-start | bytes 4194304 | tf_op jit(solution)/shard_map/all_to_all | solution.py:55
  141.4 34.7 %all-to-all-start.1 = ((bf16[32,16,2048]{2,1,0:T(8,128)(2,1)}), bf16[32,16,2048]{2,1,0:T(8,128)(2,1)}, u32[]{:S(2)}, u32[]{:S(2)}) async-start(bf16[32,16,2048]{2,1,0:T(8,128)(2,1)} %broadcast_select_fusion), calls=%async_computation.1 | async-start | bytes 4194304 | tf_op jit(solution)/shard_map/all_to_all | solution.py:69
  146.4 10.0 %copy-start.8 = (f32[16,16,2048]{2,0,1:T(8,128)S(1)}, f32[16,16,2048]{2,0,1:T(8,128)}, u32[]{:S(2)}) copy-start(f32[16,16,2048]{2,0,1:T(8,128)} %get-tuple-element.17) | copy-start | bytes 6291460
  156.4 2.5 %copy-start.7 = (f32[16,16,2048]{2,0,1:T(8,128)S(1)}, f32[16,16,2048]{2,0,1:T(8,128)}, u32[]{:S(2)}) copy-start(f32[16,16,2048]{2,0,1:T(8,128)} %get-tuple-element.18) | copy-start | bytes 6291460

commit v2 on v0

v2 whole, which is shorter than its diff:
```python
import functools
import math

import jax
import jax.numpy as jnp
from jax import lax
from jax.experimental import pallas as pl
from jax.experimental.pallas import tpu as pltpu
from jax.sharding import PartitionSpec as P

inner_rate = 0.5
outer_rate = 0.7
momentum_coef = 0.9
pseudo_lift = 64.0
weight_lift = 32.0
kernel_vmem = 60 * 1024 * 1024


def update_kernel(slots, blocks, shares, rec, master, momentum, *refs):
    new_master, new_momentum, outgoing, total = refs[-4:]
    paths, slot_total = rec.shape[0], master.shape[0]
    total[...] = jnp.zeros_like(total)
    for p in range(paths):
        total[slots[p]] += rec[p]
    for m in range(slot_total):
        mean = total[m] * shares[m]
        moved = momentum_coef * momentum[m] + mean
        new_momentum[m] = moved
        new_master[m] = master[m] - outer_rate * (mean + momentum_coef * moved)
    for p in range(paths):
        outgoing[p] = new_master[slots[p]].astype(outgoing.dtype)


def update(slots, blocks, shares, rec, master, momentum, out_width, first, earlier):
    paths, rows, width = rec.shape
    slot_total = master.shape[0]
    block = width // blocks.shape[0]
    unit = block // 2
    skipped = first // unit
    held = pl.BlockSpec((slot_total, rows, unit), lambda j, k, s, u, c: (0, 0, 2 * u[j] + k))
    passing = pl.BlockSpec((paths, rows, unit), lambda j, k, s, u, c: (0, 0, 2 * j + k))
    leaving = pl.BlockSpec((paths, rows, unit), lambda j, k, s, u, c: (0, 0, skipped + 2 * j + k))
    whole = pl.BlockSpec(memory_space=pl.ANY)
    return pl.pallas_call(
        update_kernel,
        grid_spec=pltpu.PrefetchScalarGridSpec(
            num_scalar_prefetch=3,
            grid=(blocks.shape[0], 2),
            in_specs=[passing, held, held] + [whole] * len(earlier),
            out_specs=[held, held, leaving],
            scratch_shapes=[pltpu.VMEM((slot_total, rows, unit), jnp.float32)],
        ),
        out_shape=[
            jax.ShapeDtypeStruct(master.shape, master.dtype),
            jax.ShapeDtypeStruct(momentum.shape, momentum.dtype),
            jax.ShapeDtypeStruct((paths, rows, out_width), jnp.bfloat16),
        ],
        input_output_aliases={6 + i: i for i in range(len(earlier))},
        compiler_params=pltpu.CompilerParams(vmem_limit_bytes=kernel_vmem),
        cost_estimate=pl.CostEstimate(
            flops=4 * rec.size,
            bytes_accessed=6 * rec.size + 16 * slot_total * rows * width,
            transcendentals=0,
        ),
    )(slots, blocks, shares, rec, master, momentum, *earlier)


def place_kernel(orders, which, *refs):
    *pieces, out = refs
    width = out.shape[1] // len(orders[0])
    for choice, order in enumerate(orders):

        @pl.when(which[0] == choice)
        def _():
            k = 0
            for piece in pieces:
                for i in range(piece.shape[1] // width):
                    first = order[k] * width
                    out[:, first : first + width] = piece[:, i * width : (i + 1) * width]
                    k += 1


def place(orders, which, pieces):
    rows, width = pieces[0].shape
    whole = len(orders[0]) * width
    tile = min(rows, 128)
    return pl.pallas_call(
        functools.partial(place_kernel, orders),
        grid_spec=pltpu.PrefetchScalarGridSpec(
            num_scalar_prefetch=1,
            grid=(rows // tile,),
            in_specs=[pl.BlockSpec((tile, p.shape[1]), lambda i, u: (i, 0)) for p in pieces],
            out_specs=pl.BlockSpec((tile, whole), lambda i, u: (i, 0)),
        ),
        out_shape=jax.ShapeDtypeStruct((rows, whole), pieces[0].dtype),
        compiler_params=pltpu.CompilerParams(vmem_limit_bytes=kernel_vmem),
        cost_estimate=pl.CostEstimate(
            flops=0, bytes_accessed=4 * rows * whole, transcendentals=0
        ),
    )(which, *pieces)


def back_kernel(scale, starts, weights, *refs):
    out = refs[-1]
    total = jnp.zeros(out.shape, jnp.float32)
    for i, block in enumerate(refs[:-1]):
        depth = block.shape[1]
        first = pl.multiple_of(starts[i], depth)
        total += jnp.dot(
            block[...], weights[pl.ds(first, depth), :], preferred_element_type=jnp.float32
        )
    out[...] = (total * scale).astype(out.dtype)


def input_gradient(blocks, starts, weights, scale):
    tokens = blocks[0].shape[0]
    model_width, width = weights.shape
    tile = min(tokens, 512)
    return pl.pallas_call(
        functools.partial(back_kernel, scale),
        grid_spec=pltpu.PrefetchScalarGridSpec(
            num_scalar_prefetch=1,
            grid=(tokens // tile,),
            in_specs=[pl.BlockSpec((model_width, width), lambda i, u: (0, 0))]
            + [pl.BlockSpec((tile, b.shape[1]), lambda i, u: (i, 0)) for b in blocks],
            out_specs=pl.BlockSpec((tile, width), lambda i, u: (i, 0)),
        ),
        out_shape=jax.ShapeDtypeStruct((tokens, width), jnp.bfloat16),
        compiler_params=pltpu.CompilerParams(vmem_limit_bytes=kernel_vmem),
        cost_estimate=pl.CostEstimate(
            flops=2 * tokens * model_width * width,
            bytes_accessed=2 * (tokens * model_width + model_width * width + tokens * width),
            transcendentals=0,
        ),
    )(starts, weights, *blocks)


def on_device(
    inputs, out_grad, path_weights, inner_drift, path_module, module_slot, master, momentum
):
    paths = lax.axis_size("path")
    size = lax.axis_size("shard")
    me = lax.axis_index("shard")
    model_width = path_weights.shape[2]
    width = out_grad.shape[1]
    half = width // 2
    rows = master.shape[1]
    slot_total = master.shape[0]
    unit_scale = 1.0 / math.sqrt(model_width)

    here, left, right, far = me, (me + size - 1) % size, (me + 1) % size, (me + 2) % size
    odd = lax.axis_index("path") % 2

    def stepped(block, sense):
        return lax.ppermute(
            block,
            ("path", "shard"),
            [
                (p * size + y, p * size + (y + (sense if p % 2 == 0 else -sense)) % size)
                for p in range(paths)
                for y in range(size)
            ],
        )

    chosen = path_module[:, 0]
    matches = chosen[:, None] == jnp.arange(module_slot.shape[0], dtype=jnp.int32)[None, :]
    slots = jnp.sum(jnp.where(matches, module_slot[None, :], 0), axis=1)
    shares = 1.0 / jnp.sum(
        (slots[None, :] == jnp.arange(slot_total, dtype=jnp.int32)[:, None]).astype(jnp.float32),
        axis=1,
    )

    drift = inner_drift[0]
    turned_inputs = lax.optimization_barrier(inputs.T)

    def pseudo_pieces(block, first):
        columns = block.shape[1]
        raw = jnp.dot(turned_inputs, block, preferred_element_type=jnp.float32)
        moved = lax.dynamic_slice(drift, (0, first), (drift.shape[0], columns))
        value = (moved + inner_rate * (raw * unit_scale)) * pseudo_lift
        return value.astype(jnp.float16).reshape(paths, rows, columns)

    def exchange(parts):
        whole = parts[0] if len(parts) == 1 else jnp.concatenate(parts, axis=2)
        return lax.all_to_all(whole, "path", split_axis=0, concat_axis=0, tiled=True)

    def updated(got, blocks, out_width, first, earlier):
        rec = got.astype(jnp.float32) * (1.0 / pseudo_lift)
        order = jnp.stack(blocks).astype(jnp.int32)
        return update(slots, order, shares, rec, master, momentum, out_width, first, earlier)

    first_block = stepped(out_grad, 1)
    second_block = stepped(out_grad, -1)
    got = exchange([pseudo_pieces(out_grad, here * width)])
    *earlier, outgoing = updated(got, [here], width, 0, [])
    own_sent = exchange([outgoing]).reshape(paths * rows, width)
    first_block, second_block, own_sent = lax.optimization_barrier(
        (first_block, second_block, own_sent)
    )
    far_block = stepped(first_block, 1)

    first, second = jnp.where(odd == 0, left, right), jnp.where(odd == 0, right, left)
    got = exchange(
        [pseudo_pieces(first_block, first * width), pseudo_pieces(second_block, second * width)]
    )
    even_path = (jnp.arange(paths) % 2 == 0)[:, None, None]
    left_got = jnp.where(even_path, got[:, :, :width], got[:, :, width:])
    right_got = jnp.where(even_path, got[:, :, width:], got[:, :, :width])
    *earlier, outgoing = updated(
        jnp.concatenate([left_got, right_got], axis=2), [left, right], 3 * width, 0, earlier
    )
    got = exchange([pseudo_pieces(far_block, far * width)])
    new_master, new_momentum, outgoing = updated(
        got, [far], 3 * width, 2 * width, [*earlier, outgoing]
    )
    sent = exchange([outgoing]).reshape(paths * rows, 3 * width)
    orders = [[(i + d) % size for d in (0, size - 1, 1, 2)] for i in range(size)]
    new_weights = place(orders, me.astype(jnp.int32)[None], [own_sent, sent])

    turned_weights = path_weights[0].T
    blocks = [out_grad, first_block, second_block, far_block]
    starts = jnp.stack([here, first, second, far]).astype(jnp.int32) * width
    input_grad = input_gradient(blocks, starts, turned_weights, unit_scale)
    return (input_grad, new_master, new_momentum, new_weights[None])


def solution(mesh):
    placed = (
        P("path", "shard"),
        P("path", "shard"),
        P("path", "shard", None),
        P("path", "shard", None),
        P(),
        P(),
        P(None, ("shard", "path"), None),
        P(None, ("shard", "path"), None),
    )
    return jax.shard_map(
        on_device,
        mesh=mesh,
        in_specs=placed,
        out_specs=(
            P("path", "shard"),
            P(None, ("shard", "path"), None),
            P(None, ("shard", "path"), None),
            P("path", "shard", None),
        ),
        check_vma=False,
    )
```

time: 307 us -> 140 us (0.46)
  waiting for transfers between devices: 233 us -> 38.2 us
  Pallas kernels: 0 us -> 25.4 us
  starting transfers between devices: 7.75 us -> 31.6 us
  matrix products: 31.7 us -> 14.3 us
  blocking collectives: 0 us -> 16.3 us
  between operations: 16 us -> 0.75 us
  local copies, waits for them, and re-layouts: 15.5 us -> 3.95 us
  other arithmetic: 0.84 us -> 8.47 us
    all_gather x2 -> x0, waiting for transfers between devices: 180 us -> none  [the longest x1 92.4 us: on_device(): lax.all_gather(new_master.astype(jnp.bfloat16), 'path', axis=1, tiled=True)]
    all_to_all x1 -> x4, waiting for transfers between devices: 53 us -> 27.5 us  [exchange(): lax.all_to_all(whole, 'path', split_axis=0, concat_axis=0, tiled=True)]
    pallas_call x0 -> x5, Pallas kernels: none -> 25.4 us  [the longest x3 11.9 us: update(): pl.pallas_call(update_kernel, grid_spec=pltpu.PrefetchScalarGridSpec(num_...]
    all_to_all x1 -> x4, starting transfers between devices: 7.49 us -> 26.4 us  [exchange(): lax.all_to_all(whole, 'path', split_axis=0, concat_axis=0, tiled=True)]
    dot_general x3 -> x4, matrix products: 31.7 us -> 14.3 us  [pseudo_pieces(): raw = jnp.dot(turned_inputs, block, preferred_element_type=jnp.float32)]
    all_to_all x0 -> x1, blocking collectives: none -> 16.3 us  [exchange(): lax.all_to_all(whole, 'path', split_axis=0, concat_axis=0, tiled=True)]
    ppermute x0 -> x3, waiting for transfers between devices: none -> 10.7 us  [stepped(): lax.ppermute(block, ('path', 'shard'), [(p * size + y, p * size + (y + (s...]
    dynamic_slice x1 -> x0, local copies, waits for them, and re-layouts: 7.54 us -> none  [on_device(): new_weights = lax.dynamic_slice_in_dim(whole_store, own_slot, 1, 0)]
  transfers between devices with their start and end apart: 3 -> 7, of which waited for: 3 -> 6; matrix products, arithmetic and copies ran while one was open for 5% -> 18% of each run, Pallas kernels for 0% -> 13%
where the time goes in v2:
time: 140 us; the launch traced here: 139 us
  waiting for transfers between devices  38.2 us (27%)
  starting transfers between devices  31.6 us (23%)
  Pallas kernels  25.4 us (18%)
  blocking collectives  16.3 us (12%)
  matrix products  14.3 us (10%)
  other arithmetic  8.47 us (6%)
  local copies, waits for them, and re-layouts  3.95 us (3%)
    all_to_all x4, waiting for transfers between devices, exchange(): lax.all_to_all(whole, 'path', split_axis=0, concat_axis=0, tiled=True)  27.5 us
    all_to_all x4, starting transfers between devices, exchange(): lax.all_to_all(whole, 'path', split_axis=0, concat_axis=0, tiled=True)  26.4 us
    all_to_all x1, blocking collectives, exchange(): lax.all_to_all(whole, 'path', split_axis=0, concat_axis=0, tiled=True)  16.3 us
    dot_general x4, matrix products, pseudo_pieces(): raw = jnp.dot(turned_inputs, block, preferred_element_type=jnp.float32)  14.3 us
    pallas_call x3, Pallas kernels, update(): pl.pallas_call(update_kernel, grid_spec=pltpu.PrefetchScalarGridSpec(num_...  11.9 us
    ppermute x3, waiting for transfers between devices, stepped(): lax.ppermute(block, ('path', 'shard'), [(p * size + y, p * size + (y + (s...  10.7 us
    pallas_call x1, Pallas kernels, input_gradient(): pl.pallas_call(functools.partial(back_kernel, scale), grid_spec=pltpu.Pre...  9.63 us
    ppermute x3, starting transfers between devices, stepped(): lax.ppermute(block, ('path', 'shard'), [(p * size + y, p * size + (y + (s...  5.15 us
  transfers between devices with their start and end apart: 7, of which 6 were waited for; matrix products, arithmetic and copies ran while one was open for 18% of the time, Pallas kernels for 13%

profile of v2, /device:TPU:0, one launch (start us, length us, event | category | flops | bytes accessed | tf_op | source)
XLA Modules:
  0.0 139.0 jit_solution(17101812304745541351)
XLA Ops:
  0.6 0.0 copy-start
  0.6 1.7 %collective-permute-start = (bf16[2048,512]{1,0:T(8,128)(2,1)}, bf16[2048,512]{1,0:T(8,128)(2,1)}, u32[]{:S(2)}, u32[]{:S(2)}) collective-permute-start(bf16[2048,512]{1,0:T(8,128)(2,1)} %refs_0_.1), channel_id=1, source_target_pairs={{0,1},{1,2},{2,3},{3,0},{4,7},{5,4},{6,5},{7,6},{8,9},{9,10},{10,1... | collective-permute-start | bytes 6291464 | tf_op jit(solution)/shard_map/ppermute | solution.py:155
  2.4 1.6 %collective-permute-start.1 = (bf16[2048,512]{1,0:T(8,128)(2,1)}, bf16[2048,512]{1,0:T(8,128)(2,1)}, u32[]{:S(2)}, u32[]{:S(2)}) collective-permute-start(bf16[2048,512]{1,0:T(8,128)(2,1)} %refs_0_.1), channel_id=1, source_target_pairs={{0,3},{1,0},{2,1},{3,2},{4,5},{5,6},{6,7},{7,4},{8,11},{9,8},{10,9... | collective-permute-start | bytes 6291464 | tf_op jit(solution)/shard_map/ppermute | solution.py:155
  4.0 0.0 copy-done
  4.0 0.0 copy-start.2
  4.0 0.0 copy-start.3
  4.0 4.0 %fusion.14 = f16[512,512]{1,0:T(8,128)(2,1)} fusion(bf16[512,2048]{0,1:T(8,128)(2,1)S(1)} %bitcast.59, bf16[2048,512]{1,0:T(8,128)(2,1)} %refs_0_.1, f32[1,512,2048]{2,1,0:T(8,128)} %param.11, s32[]{:T(128)S(6)} %select_n.67), kind=kOutput, calls=%fused_computation.19 | convolution fusion | flops 1074790400 | bytes 5767172 | tf_op jit(solution)/shard_map/dot_general | solution.py:178
  7.9 8.2 %all-to-all-start = ((f16[32,16,512]{2,1,0:T(8,128)(2,1)}), f16[32,16,512]{2,1,0:T(8,128)(2,1)S(1)}, u32[]{:S(2)}, u32[]{:S(2)}) async-start(f16[32,16,512]{2,1,0:T(8,128)(2,1)} %bitcast.9), calls=%async_computation | async-start | bytes 1048576 | tf_op jit(solution)/shard_map/all_to_all | solution.py:185
  16.2 0.0 copy-done.2
  16.2 0.0 copy-done.3
  16.2 0.1 select_reduce_fusion.slots
  16.3 0.0 copy-start.1
  16.3 0.1 convert_reduce_fusion
  16.4 0.6 broadcast_divide_fusion.shares
  17.0 10.9 %all-to-all-done = f16[32,16,512]{2,1,0:T(8,128)(2,1)S(1)} async-done(((f16[32,16,512]{2,1,0:T(8,128)(2,1)}), f16[32,16,512]{2,1,0:T(8,128)(2,1)S(1)}, u32[]{:S(2)}, u32[]{:S(2)}) %all-to-all-start) | async-done | bytes 524320 | tf_op jit(solution)/shard_map/all_to_all | solution.py:185
  27.9 1.1 convert_multiply_fusion.2.rec
  29.1 0.0 copy-done.1
  29.1 3.3 %shard_map.111 = (f32[16,16,2048]{2,1,0:T(8,128)}, f32[16,16,2048]{2,1,0:T(8,128)}, bf16[32,16,512]{2,1,0:T(8,128)(2,1)}) custom-call(s32[32]{0:T(128)} %copy-done.1, s32[1]{0:T(128)} %bitcast.blocks.which, f32[16]{0:T(128)} %broadcast_divide_fusion.shares, f32[32,16,512]{2,1,0:T(8,128)} %convert_multiply_fusion.2.rec, f32[16,16,2048]{2,1,0:T(8,128)} %master.5, ...), custom_call_target="tpu_custom_call" | custom-call | flops 1048576 | bytes 3670016 | tf_op jit(solution)/shard_map/pallas_call | solution.py:44
  32.3 16.3 %all_to_all.25 = bf16[32,16,512]{2,1,0:T(8,128)(2,1)} all-to-all(bf16[32,16,512]{2,1,0:T(8,128)(2,1)} %get-tuple-element.16), channel_id=1, replica_groups=mesh['path'=32,'shard'=4] {'path'}, dimensions={0} | all-to-all | bytes 1048576 | tf_op jit(solution)/shard_map/all_to_all | solution.py:185
  48.7 0.3 collective-permute-done.refs_1_
  49.0 0.0 collective-permute-done.1.refs_2_
  49.0 1.8 %collective-permute-start.2 = (bf16[2048,512]{1,0:T(8,128)(2,1)}, bf16[2048,512]{1,0:T(8,128)(2,1)}, u32[]{:S(2)}, u32[]{:S(2)}) collective-permute-start(bf16[2048,512]{1,0:T(8,128)(2,1)} %collective-permute-done.refs_1_), channel_id=1, source_target_pairs={{0,1},{1,2},{2,3},{3,0},{4,7},{5,4},{6,5},{7,6},{8,9},{9,10},{10,1... | collective-permute-start | bytes 6291464 | tf_op jit(solution)/shard_map/ppermute | solution.py:155
  50.9 3.2 %fusion.12 = f16[512,512]{1,0:T(8,128)(2,1)S(1)} fusion(bf16[2048,512]{1,0:T(8,128)(2,1)} %collective-permute-done.refs_1_, bf16[512,2048]{0,1:T(8,128)(2,1)S(1)} %bitcast.61, f32[1,512,2048]{2,1,0:T(8,128)} %param.11, s32[]{:T(128)S(6)} %select_n.70), kind=kOutput, calls=%fused_computation.17 | convolution fusion | flops 1074790400 | bytes 5767172 | tf_op jit(solution)/shard_map/dot_general | solution.py:178
  54.0 3.2 %fusion.11 = f16[512,512]{1,0:T(8,128)(2,1)S(1)} fusion(bf16[2048,512]{1,0:T(8,128)(2,1)} %collective-permute-done.1.refs_2_, bf16[512,2048]{0,1:T(8,128)(2,1)S(1)} %bitcast.58, f32[1,512,2048]{2,1,0:T(8,128)} %param.11, s32[]{:T(128)S(6)} %select_n.71), kind=kOutput, calls=%fused_computation.16 | convolution fusion | flops 1074790400 | bytes 5767172 | tf_op jit(solution)/shard_map/dot_general | solution.py:178
  57.2 1.2 pad_maximum_fusion
  58.5 8.2 %all-to-all-start.3 = ((f16[32,16,1024]{2,1,0:T(8,128)(2,1)}), f16[32,16,1024]{2,1,0:T(8,128)(2,1)S(1)}, u32[]{:S(2)}, u32[]{:S(2)}) async-start(f16[32,16,1024]{2,1,0:T(8,128)(2,1)} %pad_maximum_fusion), calls=%async_computation.3 | async-start | bytes 2097152 | tf_op jit(solution)/shard_map/all_to_all | solution.py:185
  66.7 10.4 %collective-permute-done.2.refs_3_ = bf16[2048,512]{1,0:T(8,128)(2,1)} collective-permute-done((bf16[2048,512]{1,0:T(8,128)(2,1)}, bf16[2048,512]{1,0:T(8,128)(2,1)}, u32[]{:S(2)}, u32[]{:S(2)}) %collective-permute-start.2) | collective-permute-done | bytes 2097184 | tf_op jit(solution)/shard_map/ppermute | solution.py:155
  77.0 4.0 %fusion.13 = f16[512,512]{1,0:T(8,128)(2,1)} fusion(bf16[2048,512]{1,0:T(8,128)(2,1)} %collective-permute-done.2.refs_3_, bf16[512,2048]{0,1:T(8,128)(2,1)S(1)} %bitcast.60, f32[1,512,2048]{2,1,0:T(8,128)} %param.11, s32[]{:T(128)S(6)} %select_n.68), kind=kOutput, calls=%fused_computation.18 | convolution fusion | flops 1074790400 | bytes 5767172 | tf_op jit(solution)/shard_map/dot_general | solution.py:178
  81.0 3.0 %all-to-all-done.3 = f16[32,16,1024]{2,1,0:T(8,128)(2,1)S(1)} async-done(((f16[32,16,1024]{2,1,0:T(8,128)(2,1)}), f16[32,16,1024]{2,1,0:T(8,128)(2,1)S(1)}, u32[]{:S(2)}, u32[]{:S(2)}) %all-to-all-start.3) | async-done | bytes 1048608 | tf_op jit(solution)/shard_map/all_to_all | solution.py:185
  84.0 5.3 %all-to-all-start.2 = ((f16[32,16,512]{2,1,0:T(8,128)(2,1)}), f16[32,16,512]{2,1,0:T(8,128)(2,1)}, u32[]{:S(2)}, u32[]{:S(2)}) async-start(f16[32,16,512]{2,1,0:T(8,128)(2,1)} %bitcast.65), calls=%async_computation.2 | async-start | bytes 1048576 | tf_op jit(solution)/shard_map/all_to_all | solution.py:185
  89.3 0.6 pad_add_fusion.blocks
  89.9 0.3 broadcast_select_fusion.1
  90.2 1.6 %convert_multiply_fusion.rec = f32[32,16,1024]{2,1,0:T(8,128)} fusion(f16[32,16,512]{2,1,0:T(8,128)(2,1)S(1)} %get-tuple-element.29, f16[32,16,512]{2,1,0:T(8,128)(2,1)S(1)} %get-tuple-element.28), kind=kLoop, calls=%fused_computation | loop fusion | flops 1572864 | bytes 3145728 | tf_op jit(solution)/shard_map/mul | solution.py:188
  91.9 5.3 %shard_map.113 = (f32[16,16,2048]{2,1,0:T(8,128)}, f32[16,16,2048]{2,1,0:T(8,128)}, bf16[32,16,1536]{2,1,0:T(8,128)(2,1)}) custom-call(s32[32]{0:T(128)} %copy-done.1, s32[2]{0:T(128)} %pad_add_fusion.blocks, f32[16]{0:T(128)} %broadcast_divide_fusion.shares, ...), custom_call_target="tpu_custom_call", output_to_operand_aliasing={{0}: (6, {}), {1}: (7, {})} | custom-call | flops 2097152 | bytes 7340032 | tf_op jit(solution)/shard_map/pallas_call | solution.py:44
  97.2 3.9 %all-to-all-done.2 = f16[32,16,512]{2,1,0:T(8,128)(2,1)} async-done(((f16[32,16,512]{2,1,0:T(8,128)(2,1)}), f16[32,16,512]{2,1,0:T(8,128)(2,1)}, u32[]{:S(2)}, u32[]{:S(2)}) %all-to-all-start.2) | async-done | bytes 524320 | tf_op jit(solution)/shard_map/all_to_all | solution.py:185
  101.1 2.2 %convert_multiply_fusion.1.rec = f32[32,16,512]{2,1,0:T(8,128)} fusion(f16[32,16,512]{2,1,0:T(8,128)(2,1)} %all-to-all-done.2), kind=kLoop, calls=%fused_computation.21 | loop fusion | flops 524288 | bytes 1572864 | tf_op jit(solution)/shard_map/mul | solution.py:188
  103.2 3.3 %shard_map.114 = (f32[16,16,2048]{2,1,0:T(8,128)}, f32[16,16,2048]{2,1,0:T(8,128)}, bf16[32,16,1536]{2,1,0:T(8,128)(2,1)}) custom-call(s32[32]{0:T(128)} %copy-done.1, s32[1]{0:T(128)} %bitcast.3.blocks, f32[16]{0:T(128)} %broadcast_divide_fusion.shares, ...), custom_call_target="tpu_custom_call", output_to_operand_aliasing={{0}: (6, {}), {1}: (7, {}), {2}: (8, {})} | custom-call | flops 1048576 | bytes 3670016 | tf_op jit(solution)/shard_map/pallas_call | solution.py:44
  106.5 4.7 %all-to-all-start.4 = ((bf16[32,16,1536]{2,1,0:T(8,128)(2,1)}), bf16[32,16,1536]{2,1,0:T(8,128)(2,1)}, u32[]{:S(2)}, u32[]{:S(2)}) async-start(bf16[32,16,1536]{2,1,0:T(8,128)(2,1)} %get-tuple-element.27), calls=%async_computation.4 | async-start | bytes 3145728 | tf_op jit(solution)/shard_map/all_to_all | solution.py:185
  111.2 3.9 %copy.19 = bf16[1,512,2048]{1,2,0:T(8,128)(2,1)} copy(bf16[1,512,2048]{2,1,0:T(8,128)(2,1)} %param.10) | data formatting | bytes 4194304 | tf_op args[2]
  115.1 0.6 add_multiply_fusion.starts
  115.8 9.6 %shard_map.112 = bf16[2048,512]{1,0:T(8,128)(2,1)} custom-call(s32[4]{0:T(128)} %add_multiply_fusion.starts, bf16[2048,512]{1,0:T(8,128)(2,1)} %bitcast.64, bf16[2048,512]{1,0:T(8,128)(2,1)} %refs_0_.1, bf16[2048,512]{1,0:T(8,128)(2,1)} %collective-permute-done.refs_1_, bf16[2048,512]{1,0:T(8,128)(2,1)} %collective-permute-done.1.refs_2_, ...), custom_call_target="tpu_custom_call" | custom-call | flops 4294967296 | bytes 12582912 | tf_op jit(solution)/shard_map/pallas_call | solution.py:119
  125.4 9.8 %all-to-all-done.4 = bf16[32,16,1536]{2,1,0:T(8,128)(2,1)} async-done(((bf16[32,16,1536]{2,1,0:T(8,128)(2,1)}), bf16[32,16,1536]{2,1,0:T(8,128)(2,1)}, u32[]{:S(2)}, u32[]{:S(2)}) %all-to-all-start.4) | async-done | bytes 1572896 | tf_op jit(solution)/shard_map/all_to_all | solution.py:185
  135.1 3.8 %shard_map.115 = bf16[512,2048]{1,0:T(8,128)(2,1)} custom-call(s32[1]{0:T(128)} %bitcast.blocks.which, bf16[512,512]{1,0:T(8,128)(2,1)} %bitcast.62, bf16[512,1536]{1,0:T(8,128)(2,1)} %bitcast.22.refs_1_), custom_call_target="tpu_custom_call" | custom-call | bytes 4194304 | tf_op jit(solution)/shard_map/pallas_call | solution.py:87
  (1 shorter events, 0.0 us)
Async XLA Ops:
  0.6 3.3 %copy-start = (bf16[2048,512]{1,0:T(8,128)(2,1)S(1)}, bf16[2048,512]{1,0:T(8,128)(2,1)}, u32[]{:S(2)}) copy-start(bf16[2048,512]{1,0:T(8,128)(2,1)} %param.8) | copy-start | bytes 6291460
  0.6 48.4 %collective-permute-start = (bf16[2048,512]{1,0:T(8,128)(2,1)}, bf16[2048,512]{1,0:T(8,128)(2,1)}, u32[]{:S(2)}, u32[]{:S(2)}) collective-permute-start(bf16[2048,512]{1,0:T(8,128)(2,1)} %refs_0_.1), channel_id=1, source_target_pairs={{0,1},{1,2},{2,3},{3,0},{4,7},{5,4},{6,5},{7,6},{8,9},{9,10},{10,1... | collective-permute-start | bytes 6291464 | tf_op jit(solution)/shard_map/ppermute | solution.py:155
  2.4 46.6 %collective-permute-start.1 = (bf16[2048,512]{1,0:T(8,128)(2,1)}, bf16[2048,512]{1,0:T(8,128)(2,1)}, u32[]{:S(2)}, u32[]{:S(2)}) collective-permute-start(bf16[2048,512]{1,0:T(8,128)(2,1)} %refs_0_.1), channel_id=1, source_target_pairs={{0,3},{1,0},{2,1},{3,2},{4,5},{5,6},{6,7},{7,4},{8,11},{9,8},{10,9... | collective-permute-start | bytes 6291464 | tf_op jit(solution)/shard_map/ppermute | solution.py:155
  4.0 12.2 %copy-start.2 = (s32[16]{0:T(128)S(1)}, s32[16]{0:T(128)}, u32[]{:S(2)}) copy-start(s32[16]{0:T(128)} %param.13) | copy-start | bytes 196
  4.0 12.2 %copy-start.3 = (s32[32,1]{0,1:T(1,128)S(1)}, s32[32,1]{0,1:T(1,128)}, u32[]{:S(2)}) copy-start(s32[32,1]{0,1:T(1,128)} %param.12) | copy-start | bytes 388
  7.9 20.0 %all-to-all-start = ((f16[32,16,512]{2,1,0:T(8,128)(2,1)}), f16[32,16,512]{2,1,0:T(8,128)(2,1)S(1)}, u32[]{:S(2)}, u32[]{:S(2)}) async-start(f16[32,16,512]{2,1,0:T(8,128)(2,1)} %bitcast.9), calls=%async_computation | async-start | bytes 1048576 | tf_op jit(solution)/shard_map/all_to_all | solution.py:185
  16.3 12.8 %copy-start.1 = (s32[32]{0:T(128)}, s32[32]{0:T(128)S(1)}, u32[]{:S(2)}) copy-start(s32[32]{0:T(128)S(1)} %select_reduce_fusion.slots) | copy-start | bytes 388
  49.0 28.0 %collective-permute-start.2 = (bf16[2048,512]{1,0:T(8,128)(2,1)}, bf16[2048,512]{1,0:T(8,128)(2,1)}, u32[]{:S(2)}, u32[]{:S(2)}) collective-permute-start(bf16[2048,512]{1,0:T(8,128)(2,1)} %collective-permute-done.refs_1_), channel_id=1, source_target_pairs={{0,1},{1,2},{2,3},{3,0},{4,7},{5,4},{6,5},{7,6},{8,9},{9,10},{10,1... | collective-permute-start | bytes 6291464 | tf_op jit(solution)/shard_map/ppermute | solution.py:155
  58.5 25.5 %all-to-all-start.3 = ((f16[32,16,1024]{2,1,0:T(8,128)(2,1)}), f16[32,16,1024]{2,1,0:T(8,128)(2,1)S(1)}, u32[]{:S(2)}, u32[]{:S(2)}) async-start(f16[32,16,1024]{2,1,0:T(8,128)(2,1)} %pad_maximum_fusion), calls=%async_computation.3 | async-start | bytes 2097152 | tf_op jit(solution)/shard_map/all_to_all | solution.py:185
  84.0 17.1 %all-to-all-start.2 = ((f16[32,16,512]{2,1,0:T(8,128)(2,1)}), f16[32,16,512]{2,1,0:T(8,128)(2,1)}, u32[]{:S(2)}, u32[]{:S(2)}) async-start(f16[32,16,512]{2,1,0:T(8,128)(2,1)} %bitcast.65), calls=%async_computation.2 | async-start | bytes 1048576 | tf_op jit(solution)/shard_map/all_to_all | solution.py:185
  106.5 28.6 %all-to-all-start.4 = ((bf16[32,16,1536]{2,1,0:T(8,128)(2,1)}), bf16[32,16,1536]{2,1,0:T(8,128)(2,1)}, u32[]{:S(2)}, u32[]{:S(2)}) async-start(bf16[32,16,1536]{2,1,0:T(8,128)(2,1)} %get-tuple-element.27), calls=%async_computation.4 | async-start | bytes 3145728 | tf_op jit(solution)/shard_map/all_to_all | solution.py:185

commit v3 on v2

--- a/solution.py
+++ b/solution.py
@@ -13,7 +13,8 @@
 momentum_coef = 0.9
 pseudo_lift = 64.0
 weight_lift = 32.0
-kernel_vmem = 60 * 1024 * 1024
+kernel_vmem = 24 * 1024 * 1024
+small_vmem = 10 * 1024 * 1024
 
 
 def update_kernel(slots, blocks, shares, rec, master, momentum, *refs):
@@ -31,16 +32,18 @@
         outgoing[p] = new_master[slots[p]].astype(outgoing.dtype)
 
 
-def update(slots, blocks, shares, rec, master, momentum, out_width, first, earlier):
+def update(slots, blocks, shares, rec, master, momentum, earlier, out_width, first):
     paths, rows, width = rec.shape
     slot_total = master.shape[0]
-    block = width // blocks.shape[0]
-    unit = block // 2
+    unit = width // blocks.shape[0] // 2
     skipped = first // unit
     held = pl.BlockSpec((slot_total, rows, unit), lambda j, k, s, u, c: (0, 0, 2 * u[j] + k))
     passing = pl.BlockSpec((paths, rows, unit), lambda j, k, s, u, c: (0, 0, 2 * j + k))
     leaving = pl.BlockSpec((paths, rows, unit), lambda j, k, s, u, c: (0, 0, skipped + 2 * j + k))
     whole = pl.BlockSpec(memory_space=pl.ANY)
+    master, momentum, *earlier = [
+        pltpu.with_memory_space_constraint(x, pltpu.HBM) for x in (master, momentum, *earlier)
+    ]
     return pl.pallas_call(
         update_kernel,
         grid_spec=pltpu.PrefetchScalarGridSpec(
@@ -51,12 +54,12 @@
             scratch_shapes=[pltpu.VMEM((slot_total, rows, unit), jnp.float32)],
         ),
         out_shape=[
-            jax.ShapeDtypeStruct(master.shape, master.dtype),
-            jax.ShapeDtypeStruct(momentum.shape, momentum.dtype),
-            jax.ShapeDtypeStruct((paths, rows, out_width), jnp.bfloat16),
+            pltpu.HBM(master.shape, master.dtype),
+            pltpu.HBM(momentum.shape, momentum.dtype),
+            pltpu.HBM((paths, rows, out_width), jnp.bfloat16),
         ],
         input_output_aliases={6 + i: i for i in range(len(earlier))},
-        compiler_params=pltpu.CompilerParams(vmem_limit_bytes=kernel_vmem),
+        compiler_params=pltpu.CompilerParams(vmem_limit_bytes=small_vmem),
         cost_estimate=pl.CostEstimate(
             flops=4 * rec.size,
             bytes_accessed=6 * rec.size + 16 * slot_total * rows * width,
@@ -83,7 +86,7 @@
 def place(orders, which, pieces):
     rows, width = pieces[0].shape
     whole = len(orders[0]) * width
-    tile = min(rows, 128)
+    tile = rows // 2
     return pl.pallas_call(
         functools.partial(place_kernel, orders),
         grid_spec=pltpu.PrefetchScalarGridSpec(
@@ -184,15 +187,15 @@
         whole = parts[0] if len(parts) == 1 else jnp.concatenate(parts, axis=2)
         return lax.all_to_all(whole, "path", split_axis=0, concat_axis=0, tiled=True)
 
-    def updated(got, blocks, out_width, first, earlier):
+    def updated(got, blocks, earlier, out_width, first=0):
         rec = got.astype(jnp.float32) * (1.0 / pseudo_lift)
         order = jnp.stack(blocks).astype(jnp.int32)
-        return update(slots, order, shares, rec, master, momentum, out_width, first, earlier)
+        return update(slots, order, shares, rec, master, momentum, earlier, out_width, first)
 
     first_block = stepped(out_grad, 1)
     second_block = stepped(out_grad, -1)
     got = exchange([pseudo_pieces(out_grad, here * width)])
-    *earlier, outgoing = updated(got, [here], width, 0, [])
+    *earlier, outgoing = updated(got, [here], [], width)
     own_sent = exchange([outgoing]).reshape(paths * rows, width)
     first_block, second_block, own_sent = lax.optimization_barrier(
         (first_block, second_block, own_sent)
@@ -203,24 +206,28 @@
     got = exchange(
         [pseudo_pieces(first_block, first * width), pseudo_pieces(second_block, second * width)]
     )
+    far_pieces = pseudo_pieces(far_block, far * width)
+    got, far_pieces = lax.optimization_barrier((got, far_pieces))
+    far_got = exchange([far_pieces])
     even_path = (jnp.arange(paths) % 2 == 0)[:, None, None]
     left_got = jnp.where(even_path, got[:, :, :width], got[:, :, width:])
     right_got = jnp.where(even_path, got[:, :, width:], got[:, :, :width])
     *earlier, outgoing = updated(
-        jnp.concatenate([left_got, right_got], axis=2), [left, right], 3 * width, 0, earlier
-    )
-    got = exchange([pseudo_pieces(far_block, far * width)])
+        jnp.concatenate([left_got, right_got], axis=2), [left, right], earlier, 3 * width
+    )
     new_master, new_momentum, outgoing = updated(
-        got, [far], 3 * width, 2 * width, [*earlier, outgoing]
+        far_got, [far], [*earlier, outgoing], 3 * width, 2 * width
     )
     sent = exchange([outgoing]).reshape(paths * rows, 3 * width)
+
+    blocks = [out_grad, first_block, second_block, far_block]
+    starts = jnp.stack([here, first, second, far]).astype(jnp.int32) * width
+    input_grad = input_gradient(blocks, starts, path_weights[0].T, unit_scale)
+    sent, new_master, new_momentum, input_grad = lax.optimization_barrier(
+        (sent, new_master, new_momentum, input_grad)
+    )
     orders = [[(i + d) % size for d in (0, size - 1, 1, 2)] for i in range(size)]
     new_weights = place(orders, me.astype(jnp.int32)[None], [own_sent, sent])
-
-    turned_weights = path_weights[0].T
-    blocks = [out_grad, first_block, second_block, far_block]
-    starts = jnp.stack([here, first, second, far]).astype(jnp.int32) * width
-    input_grad = input_gradient(blocks, starts, turned_weights, unit_scale)
     return (input_grad, new_master, new_momentum, new_weights[None])
 
 

time: 140 us -> 136 us (0.971)
  other arithmetic: 8.47 us -> 3.71 us
  Pallas kernels: 25.4 us -> 21.8 us
  local copies, waits for them, and re-layouts: 3.95 us -> 7.13 us
  waiting for transfers between devices: 38.2 us -> 40.6 us
    mul x3, other arithmetic: 4.89 us -> 0.57 us  [updated(): rec = got.astype(jnp.float32) * (1.0 / pseudo_lift)]
    unnamed x9 -> x11, local copies, waits for them, and re-layouts: 3.95 us -> 7.13 us
    ppermute x3, waiting for transfers between devices: 10.7 us -> 12.5 us  [stepped(): lax.ppermute(block, ('path', 'shard'), [(p * size + y, p * size + (y + (s...]
    pallas_call x1, Pallas kernels: 9.63 us -> 8.1 us  [input_gradient(): pl.pallas_call(functools.partial(back_kernel, scale), grid_spec=pltpu.Pre...]
  transfers between devices with their start and end apart: 7 -> 7, of which waited for: 6 -> 6; matrix products, arithmetic and copies ran while one was open for 18% -> 16% of each run, Pallas kernels for 13% -> 12%
where the time goes in v3:
time: 136 us; the launch traced here: 135 us
  waiting for transfers between devices  40.6 us (30%)
  starting transfers between devices  31.5 us (23%)
  Pallas kernels  21.8 us (16%)
  blocking collectives  15.6 us (11%)
  matrix products  14.3 us (11%)
  local copies, waits for them, and re-layouts  7.13 us (5%)
  other arithmetic  3.71 us (3%)
    all_to_all x4, waiting for transfers between devices, exchange(): lax.all_to_all(whole, 'path', split_axis=0, concat_axis=0, tiled=True)  28.1 us
    all_to_all x4, starting transfers between devices, exchange(): lax.all_to_all(whole, 'path', split_axis=0, concat_axis=0, tiled=True)  26.3 us
    all_to_all x1, blocking collectives, exchange(): lax.all_to_all(whole, 'path', split_axis=0, concat_axis=0, tiled=True)  15.6 us
    dot_general x4, matrix products, pseudo_pieces(): raw = jnp.dot(turned_inputs, block, preferred_element_type=jnp.float32)  14.3 us
    ppermute x3, waiting for transfers between devices, stepped(): lax.ppermute(block, ('path', 'shard'), [(p * size + y, p * size + (y + (s...  12.5 us
    pallas_call x3, Pallas kernels, update(): pl.pallas_call(update_kernel, grid_spec=pltpu.PrefetchScalarGridSpec(num_...  11.1 us
    pallas_call x1, Pallas kernels, input_gradient(): pl.pallas_call(functools.partial(back_kernel, scale), grid_spec=pltpu.Pre...  8.1 us
    unnamed x11, local copies, waits for them, and re-layouts  7.13 us
  transfers between devices with their start and end apart: 7, of which 6 were waited for; matrix products, arithmetic and copies ran while one was open for 16% of the time, Pallas kernels for 12%

profile of v3, /device:TPU:0, one launch (start us, length us, event | category | flops | bytes accessed | tf_op | source)
XLA Modules:
  0.0 135.4 jit_solution(7135844145401771303)
XLA Ops:
  0.6 0.0 copy-start
  0.6 1.7 %collective-permute-start = (bf16[2048,512]{1,0:T(8,128)(2,1)}, bf16[2048,512]{1,0:T(8,128)(2,1)}, u32[]{:S(2)}, u32[]{:S(2)}) collective-permute-start(bf16[2048,512]{1,0:T(8,128)(2,1)} %refs_0_.1), channel_id=1, source_target_pairs={{0,1},{1,2},{2,3},{3,0},{4,7},{5,4},{6,5},{7,6},{8,9},{9,10},{10,1... | collective-permute-start | bytes 6291464 | tf_op jit(solution)/shard_map/ppermute | solution.py:158
  2.4 1.6 %collective-permute-start.1 = (bf16[2048,512]{1,0:T(8,128)(2,1)}, bf16[2048,512]{1,0:T(8,128)(2,1)}, u32[]{:S(2)}, u32[]{:S(2)}) collective-permute-start(bf16[2048,512]{1,0:T(8,128)(2,1)} %refs_0_.1), channel_id=1, source_target_pairs={{0,3},{1,0},{2,1},{3,2},{4,5},{5,6},{6,7},{7,4},{8,11},{9,8},{10,9... | collective-permute-start | bytes 6291464 | tf_op jit(solution)/shard_map/ppermute | solution.py:158
  4.0 0.0 copy-done
  4.0 0.0 copy-start.3
  4.0 0.0 copy-start.4
  4.0 4.0 %fusion.14 = f16[512,512]{1,0:T(8,128)(2,1)} fusion(bf16[512,2048]{0,1:T(8,128)(2,1)S(1)} %bitcast.59, bf16[2048,512]{1,0:T(8,128)(2,1)} %refs_0_.1, f32[1,512,2048]{2,1,0:T(8,128)} %param.11, s32[]{:T(128)S(6)} %select_n.67), kind=kOutput, calls=%fused_computation.19 | convolution fusion | flops 1074790400 | bytes 5767172 | tf_op jit(solution)/shard_map/dot_general | solution.py:181
  7.9 8.2 %all-to-all-start = ((f16[32,16,512]{2,1,0:T(8,128)(2,1)}), f16[32,16,512]{2,1,0:T(8,128)(2,1)S(1)}, u32[]{:S(2)}, u32[]{:S(2)}) async-start(f16[32,16,512]{2,1,0:T(8,128)(2,1)} %bitcast.6), calls=%async_computation | async-start | bytes 1048576 | tf_op jit(solution)/shard_map/all_to_all | solution.py:188
  16.2 0.0 copy-done.3
  16.2 0.0 copy-done.4
  16.2 0.1 select_reduce_fusion.slots
  16.3 0.1 convert_reduce_fusion
  16.4 11.5 %all-to-all-done = f16[32,16,512]{2,1,0:T(8,128)(2,1)S(1)} async-done(((f16[32,16,512]{2,1,0:T(8,128)(2,1)}), f16[32,16,512]{2,1,0:T(8,128)(2,1)S(1)}, u32[]{:S(2)}, u32[]{:S(2)}) %all-to-all-start) | async-done | bytes 524320 | tf_op jit(solution)/shard_map/all_to_all | solution.py:188
  27.9 0.1 convert_multiply_fusion.2.rec
  28.1 3.0 %shard_map.111 = (f32[16,16,2048]{2,1,0:T(8,128)}, f32[16,16,2048]{2,1,0:T(8,128)}, bf16[32,16,512]{2,1,0:T(8,128)(2,1)}) custom-call(s32[32]{0:T(128)S(1)} %select_reduce_fusion.slots, s32[1]{0:T(128)} %bitcast.3.blocks.which, f32[16]{0:T(128)S(1)} %broadcast_divide_fusion.shares, f32[32,16,512]{2,1,0:T(8,128)S(1)} %convert_multiply_fusion.2.rec, ...), custom_call_target="tpu_custom_call" | custom-call | flops 1048576 | bytes 3670016 | tf_op jit(solution)/shard_map/pallas_call | solution.py:47
  31.1 15.6 %all_to_all.25 = bf16[32,16,512]{2,1,0:T(8,128)(2,1)S(1)} all-to-all(bf16[32,16,512]{2,1,0:T(8,128)(2,1)} %get-tuple-element.22), channel_id=1, replica_groups=mesh['path'=32,'shard'=4] {'path'}, dimensions={0} | all-to-all | bytes 1048576 | tf_op jit(solution)/shard_map/all_to_all | solution.py:188
  46.7 2.3 %collective-permute-done.refs_1_ = bf16[2048,512]{1,0:T(8,128)(2,1)} collective-permute-done((bf16[2048,512]{1,0:T(8,128)(2,1)}, bf16[2048,512]{1,0:T(8,128)(2,1)}, u32[]{:S(2)}, u32[]{:S(2)}) %collective-permute-start) | collective-permute-done | bytes 2097184 | tf_op jit(solution)/shard_map/ppermute | solution.py:158
  49.0 0.0 collective-permute-done.1.refs_2_
  49.0 1.8 %collective-permute-start.2 = (bf16[2048,512]{1,0:T(8,128)(2,1)}, bf16[2048,512]{1,0:T(8,128)(2,1)}, u32[]{:S(2)}, u32[]{:S(2)}) collective-permute-start(bf16[2048,512]{1,0:T(8,128)(2,1)} %collective-permute-done.refs_1_), channel_id=1, source_target_pairs={{0,1},{1,2},{2,3},{3,0},{4,7},{5,4},{6,5},{7,6},{8,9},{9,10},{10,1... | collective-permute-start | bytes 6291464 | tf_op jit(solution)/shard_map/ppermute | solution.py:158
  50.9 3.2 %fusion.13 = f16[512,512]{1,0:T(8,128)(2,1)S(1)} fusion(bf16[2048,512]{1,0:T(8,128)(2,1)} %collective-permute-done.refs_1_, bf16[512,2048]{0,1:T(8,128)(2,1)S(1)} %bitcast.60, f32[1,512,2048]{2,1,0:T(8,128)} %param.11, s32[]{:T(128)S(6)} %select_n.66), kind=kOutput, calls=%fused_computation.18 | convolution fusion | flops 1074790400 | bytes 5767172 | tf_op jit(solution)/shard_map/dot_general | solution.py:181
  54.0 3.2 %fusion.12 = f16[512,512]{1,0:T(8,128)(2,1)S(1)} fusion(bf16[2048,512]{1,0:T(8,128)(2,1)} %collective-permute-done.1.refs_2_, bf16[512,2048]{0,1:T(8,128)(2,1)S(1)} %bitcast.61, f32[1,512,2048]{2,1,0:T(8,128)} %param.11, s32[]{:T(128)S(6)} %select_n.69), kind=kOutput, calls=%fused_computation.17 | convolution fusion | flops 1074790400 | bytes 5767172 | tf_op jit(solution)/shard_map/dot_general | solution.py:181
  57.2 1.2 pad_maximum_fusion
  58.5 8.3 %all-to-all-start.2 = ((f16[32,16,1024]{2,1,0:T(8,128)(2,1)}), f16[32,16,1024]{2,1,0:T(8,128)(2,1)}, u32[]{:S(2)}, u32[]{:S(2)}) async-start(f16[32,16,1024]{2,1,0:T(8,128)(2,1)} %pad_maximum_fusion), calls=%async_computation.2 | async-start | bytes 2097152 | tf_op jit(solution)/shard_map/all_to_all | solution.py:188
  66.8 10.2 %collective-permute-done.2.refs_3_ = bf16[2048,512]{1,0:T(8,128)(2,1)} collective-permute-done((bf16[2048,512]{1,0:T(8,128)(2,1)}, bf16[2048,512]{1,0:T(8,128)(2,1)}, u32[]{:S(2)}, u32[]{:S(2)}) %collective-permute-start.2) | collective-permute-done | bytes 2097184 | tf_op jit(solution)/shard_map/ppermute | solution.py:158
  77.0 4.0 %fusion.11 = f16[512,512]{1,0:T(8,128)(2,1)} fusion(bf16[2048,512]{1,0:T(8,128)(2,1)} %collective-permute-done.2.refs_3_, bf16[512,2048]{0,1:T(8,128)(2,1)S(1)} %bitcast.58, f32[1,512,2048]{2,1,0:T(8,128)} %param.11, s32[]{:T(128)S(6)} %select_n.70), kind=kOutput, calls=%fused_computation.16 | convolution fusion | flops 1074790400 | bytes 5767172 | tf_op jit(solution)/shard_map/dot_general | solution.py:181
  81.0 3.1 %all-to-all-done.2 = f16[32,16,1024]{2,1,0:T(8,128)(2,1)} async-done(((f16[32,16,1024]{2,1,0:T(8,128)(2,1)}), f16[32,16,1024]{2,1,0:T(8,128)(2,1)}, u32[]{:S(2)}, u32[]{:S(2)}) %all-to-all-start.2) | async-done | bytes 1048608 | tf_op jit(solution)/shard_map/all_to_all | solution.py:188
  84.1 5.1 %all-to-all-start.3 = ((f16[32,16,512]{2,1,0:T(8,128)(2,1)}), f16[32,16,512]{2,1,0:T(8,128)(2,1)S(1)}, u32[]{:S(2)}, u32[]{:S(2)}) async-start(f16[32,16,512]{2,1,0:T(8,128)(2,1)} %bitcast.65), calls=%async_computation.3 | async-start | bytes 1048576 | tf_op jit(solution)/shard_map/all_to_all | solution.py:188
  89.2 0.1 pad_add_fusion.blocks
  89.3 1.5 %broadcast_select_fusion.1 = (f16[32,16,512]{2,1,0:T(8,128)(2,1)S(1)}, f16[32,16,512]{2,1,0:T(8,128)(2,1)S(1)}) fusion(pred[32]{0:T(512)(128)(4,1)S(1)} %fusion.15, f16[32,16,1024]{2,1,0:T(8,128)(2,1)} %all-to-all-done.2), kind=kLoop, calls=%fused_computation.24 | loop fusion | flops 524288 | bytes 2097184 | tf_op jit(solution)/shard_map/jit(_where)/select_n | solution.py:213
  90.8 0.3 convert_multiply_fusion.rec
  91.1 5.0 %shard_map.112 = (f32[16,16,2048]{2,1,0:T(8,128)}, f32[16,16,2048]{2,1,0:T(8,128)}, bf16[32,16,1536]{2,1,0:T(8,128)(2,1)}) custom-call(s32[32]{0:T(128)S(1)} %select_reduce_fusion.slots, s32[2]{0:T(128)S(1)} %pad_add_fusion.blocks, f32[16]{0:T(128)S(1)} %broadcast_divide_fusion.shares, ...), custom_call_target="tpu_custom_call", output_to_operand_aliasing={{0}: (6, {}), {1}: (7, {})} | custom-call | flops 2097152 | bytes 7340032 | tf_op jit(solution)/shard_map/pallas_call | solution.py:47
  96.1 4.8 %all-to-all-done.3 = f16[32,16,512]{2,1,0:T(8,128)(2,1)S(1)} async-done(((f16[32,16,512]{2,1,0:T(8,128)(2,1)}), f16[32,16,512]{2,1,0:T(8,128)(2,1)S(1)}, u32[]{:S(2)}, u32[]{:S(2)}) %all-to-all-start.3) | async-done | bytes 524320 | tf_op jit(solution)/shard_map/all_to_all | solution.py:188
  100.9 0.1 convert_multiply_fusion.1.rec
  101.1 3.1 %shard_map.113 = (f32[16,16,2048]{2,1,0:T(8,128)}, f32[16,16,2048]{2,1,0:T(8,128)}, bf16[32,16,1536]{2,1,0:T(8,128)(2,1)}) custom-call(s32[32]{0:T(128)S(1)} %select_reduce_fusion.slots, s32[1]{0:T(128)} %bitcast.1.blocks, f32[16]{0:T(128)S(1)} %broadcast_divide_fusion.shares, ...), custom_call_target="tpu_custom_call", output_to_operand_aliasing={{0}: (6, {}), {1}: (7, {}), {2}: (8, {})} | custom-call | flops 1048576 | bytes 3670016 | tf_op jit(solution)/shard_map/pallas_call | solution.py:47
  104.2 4.7 %all-to-all-start.4 = ((bf16[32,16,1536]{2,1,0:T(8,128)(2,1)}), bf16[32,16,1536]{2,1,0:T(8,128)(2,1)}, u32[]{:S(2)}, u32[]{:S(2)}) async-start(bf16[32,16,1536]{2,1,0:T(8,128)(2,1)} %get-tuple-element.32), calls=%async_computation.4 | async-start | bytes 3145728 | tf_op jit(solution)/shard_map/all_to_all | solution.py:188
  108.9 3.9 %copy.20 = bf16[1,512,2048]{1,2,0:T(8,128)(2,1)} copy(bf16[1,512,2048]{2,1,0:T(8,128)(2,1)} %param.10) | data formatting | bytes 4194304 | tf_op args[2]
  112.9 0.1 add_multiply_fusion.starts
  112.9 0.0 copy-start.1
  112.9 1.6 %copy-done.1 = bf16[2048,512]{1,0:T(8,128)(2,1)S(1)} copy-done((bf16[2048,512]{1,0:T(8,128)(2,1)S(1)}, bf16[2048,512]{1,0:T(8,128)(2,1)}, u32[]{:S(2)}) %copy-start.1) | copy-done | bytes 2097176
  114.5 0.0 copy-start.2
  114.5 1.6 %copy-done.2 = bf16[1,512,2048]{1,2,0:T(8,128)(2,1)S(1)} copy-done((bf16[1,512,2048]{1,2,0:T(8,128)(2,1)S(1)}, bf16[1,512,2048]{1,2,0:T(8,128)(2,1)}, u32[]{:S(2)}) %copy-start.2) | copy-done | bytes 2097176
  116.1 8.1 %shard_map.114 = bf16[2048,512]{1,0:T(8,128)(2,1)} custom-call(s32[4]{0:T(128)S(1)} %add_multiply_fusion.starts, bf16[2048,512]{1,0:T(8,128)(2,1)S(1)} %bitcast.63, bf16[2048,512]{1,0:T(8,128)(2,1)S(1)} %copy-done.1, bf16[2048,512]{1,0:T(8,128)(2,1)} %collective-permute-done.refs_1_, bf16[2048,512]{1,0:T(8,128)(2,1)} %collective-permute-done.1.refs_2_, ...), custom_call_target="tpu_custom_call" | custom-call | flops 4294967296 | bytes 12582912 | tf_op jit(solution)/shard_map/pallas_call | solution.py:122
  124.2 8.6 %all-to-all-done.4 = bf16[32,16,1536]{2,1,0:T(8,128)(2,1)} async-done(((bf16[32,16,1536]{2,1,0:T(8,128)(2,1)}), bf16[32,16,1536]{2,1,0:T(8,128)(2,1)}, u32[]{:S(2)}, u32[]{:S(2)}) %all-to-all-start.4) | async-done | bytes 1572896 | tf_op jit(solution)/shard_map/all_to_all | solution.py:188
  132.9 2.5 %shard_map.115 = bf16[512,2048]{1,0:T(8,128)(2,1)} custom-call(s32[1]{0:T(128)} %bitcast.3.blocks.which, bf16[512,512]{1,0:T(8,128)(2,1)S(1)} %bitcast.62, bf16[512,1536]{1,0:T(8,128)(2,1)} %bitcast.18.refs_1_), custom_call_target="tpu_custom_call" | custom-call | bytes 4194304 | tf_op jit(solution)/shard_map/pallas_call | solution.py:90
  (2 shorter events, 0.0 us)
Async XLA Ops:
  0.6 3.3 %copy-start = (bf16[2048,512]{1,0:T(8,128)(2,1)S(1)}, bf16[2048,512]{1,0:T(8,128)(2,1)}, u32[]{:S(2)}) copy-start(bf16[2048,512]{1,0:T(8,128)(2,1)} %param.8) | copy-start | bytes 6291460
  0.6 48.4 %collective-permute-start = (bf16[2048,512]{1,0:T(8,128)(2,1)}, bf16[2048,512]{1,0:T(8,128)(2,1)}, u32[]{:S(2)}, u32[]{:S(2)}) collective-permute-start(bf16[2048,512]{1,0:T(8,128)(2,1)} %refs_0_.1), channel_id=1, source_target_pairs={{0,1},{1,2},{2,3},{3,0},{4,7},{5,4},{6,5},{7,6},{8,9},{9,10},{10,1... | collective-permute-start | bytes 6291464 | tf_op jit(solution)/shard_map/ppermute | solution.py:158
  2.4 46.6 %collective-permute-start.1 = (bf16[2048,512]{1,0:T(8,128)(2,1)}, bf16[2048,512]{1,0:T(8,128)(2,1)}, u32[]{:S(2)}, u32[]{:S(2)}) collective-permute-start(bf16[2048,512]{1,0:T(8,128)(2,1)} %refs_0_.1), channel_id=1, source_target_pairs={{0,3},{1,0},{2,1},{3,2},{4,5},{5,6},{6,7},{7,4},{8,11},{9,8},{10,9... | collective-permute-start | bytes 6291464 | tf_op jit(solution)/shard_map/ppermute | solution.py:158
  4.0 12.2 %copy-start.3 = (s32[16]{0:T(128)S(1)}, s32[16]{0:T(128)}, u32[]{:S(2)}) copy-start(s32[16]{0:T(128)} %param.13) | copy-start | bytes 196
  4.0 12.2 %copy-start.4 = (s32[32,1]{0,1:T(1,128)S(1)}, s32[32,1]{0,1:T(1,128)}, u32[]{:S(2)}) copy-start(s32[32,1]{0,1:T(1,128)} %param.12) | copy-start | bytes 388
  7.9 20.0 %all-to-all-start = ((f16[32,16,512]{2,1,0:T(8,128)(2,1)}), f16[32,16,512]{2,1,0:T(8,128)(2,1)S(1)}, u32[]{:S(2)}, u32[]{:S(2)}) async-start(f16[32,16,512]{2,1,0:T(8,128)(2,1)} %bitcast.6), calls=%async_computation | async-start | bytes 1048576 | tf_op jit(solution)/shard_map/all_to_all | solution.py:188
  49.0 28.0 %collective-permute-start.2 = (bf16[2048,512]{1,0:T(8,128)(2,1)}, bf16[2048,512]{1,0:T(8,128)(2,1)}, u32[]{:S(2)}, u32[]{:S(2)}) collective-permute-start(bf16[2048,512]{1,0:T(8,128)(2,1)} %collective-permute-done.refs_1_), channel_id=1, source_target_pairs={{0,1},{1,2},{2,3},{3,0},{4,7},{5,4},{6,5},{7,6},{8,9},{9,10},{10,1... | collective-permute-start | bytes 6291464 | tf_op jit(solution)/shard_map/ppermute | solution.py:158
  58.5 25.6 %all-to-all-start.2 = ((f16[32,16,1024]{2,1,0:T(8,128)(2,1)}), f16[32,16,1024]{2,1,0:T(8,128)(2,1)}, u32[]{:S(2)}, u32[]{:S(2)}) async-start(f16[32,16,1024]{2,1,0:T(8,128)(2,1)} %pad_maximum_fusion), calls=%async_computation.2 | async-start | bytes 2097152 | tf_op jit(solution)/shard_map/all_to_all | solution.py:188
  84.1 16.9 %all-to-all-start.3 = ((f16[32,16,512]{2,1,0:T(8,128)(2,1)}), f16[32,16,512]{2,1,0:T(8,128)(2,1)S(1)}, u32[]{:S(2)}, u32[]{:S(2)}) async-start(f16[32,16,512]{2,1,0:T(8,128)(2,1)} %bitcast.65), calls=%async_computation.3 | async-start | bytes 1048576 | tf_op jit(solution)/shard_map/all_to_all | solution.py:188
  104.2 28.6 %all-to-all-start.4 = ((bf16[32,16,1536]{2,1,0:T(8,128)(2,1)}), bf16[32,16,1536]{2,1,0:T(8,128)(2,1)}, u32[]{:S(2)}, u32[]{:S(2)}) async-start(bf16[32,16,1536]{2,1,0:T(8,128)(2,1)} %get-tuple-element.32), calls=%async_computation.4 | async-start | bytes 3145728 | tf_op jit(solution)/shard_map/all_to_all | solution.py:188
  112.9 1.6 %copy-start.1 = (bf16[2048,512]{1,0:T(8,128)(2,1)S(1)}, bf16[2048,512]{1,0:T(8,128)(2,1)}, u32[]{:S(2)}) copy-start(bf16[2048,512]{1,0:T(8,128)(2,1)} %refs_0_.1) | copy-start | bytes 6291460
  114.5 1.6 %copy-start.2 = (bf16[1,512,2048]{1,2,0:T(8,128)(2,1)S(1)}, bf16[1,512,2048]{1,2,0:T(8,128)(2,1)}, u32[]{:S(2)}) copy-start(bf16[1,512,2048]{1,2,0:T(8,128)(2,1)} %copy.20) | copy-start | bytes 6291460

commit v4 on v3

--- a/solution.py
+++ b/solution.py
@@ -17,8 +17,8 @@
 small_vmem = 10 * 1024 * 1024
 
 
-def update_kernel(slots, blocks, shares, rec, master, momentum, *refs):
-    new_master, new_momentum, outgoing, total = refs[-4:]
+def update_kernel(stores, passes_on, slots, blocks, shares, rec, master, momentum, *refs):
+    *results, total = refs[-(2 * stores + passes_on + 1) :]
     paths, slot_total = rec.shape[0], master.shape[0]
     total[...] = jnp.zeros_like(total)
     for p in range(paths):
@@ -26,13 +26,17 @@
     for m in range(slot_total):
         mean = total[m] * shares[m]
         moved = momentum_coef * momentum[m] + mean
-        new_momentum[m] = moved
-        new_master[m] = master[m] - outer_rate * (mean + momentum_coef * moved)
-    for p in range(paths):
-        outgoing[p] = new_master[slots[p]].astype(outgoing.dtype)
-
-
-def update(slots, blocks, shares, rec, master, momentum, earlier, out_width, first):
+        fresh = master[m] - outer_rate * (mean + momentum_coef * moved)
+        total[m] = fresh
+        if stores:
+            results[0][m] = fresh
+            results[1][m] = moved
+    if passes_on:
+        for p in range(paths):
+            results[-1][p] = total[slots[p]].astype(results[-1].dtype)
+
+
+def update(slots, blocks, shares, rec, master, momentum, earlier, out_width=0, first=0, stores=True):
     paths, rows, width = rec.shape
     slot_total = master.shape[0]
     unit = width // blocks.shape[0] // 2
@@ -41,29 +45,90 @@
     passing = pl.BlockSpec((paths, rows, unit), lambda j, k, s, u, c: (0, 0, 2 * j + k))
     leaving = pl.BlockSpec((paths, rows, unit), lambda j, k, s, u, c: (0, 0, skipped + 2 * j + k))
     whole = pl.BlockSpec(memory_space=pl.ANY)
+    results = [pltpu.HBM(x.shape, x.dtype) for x in (master, momentum)] if stores else []
+    if out_width:
+        results.append(pltpu.HBM((paths, rows, out_width), jnp.bfloat16))
     master, momentum, *earlier = [
         pltpu.with_memory_space_constraint(x, pltpu.HBM) for x in (master, momentum, *earlier)
     ]
     return pl.pallas_call(
-        update_kernel,
+        functools.partial(update_kernel, stores, out_width > 0),
         grid_spec=pltpu.PrefetchScalarGridSpec(
             num_scalar_prefetch=3,
             grid=(blocks.shape[0], 2),
             in_specs=[passing, held, held] + [whole] * len(earlier),
-            out_specs=[held, held, leaving],
+            out_specs=[held] * (2 * stores) + [leaving] * (out_width > 0),
             scratch_shapes=[pltpu.VMEM((slot_total, rows, unit), jnp.float32)],
         ),
-        out_shape=[
-            pltpu.HBM(master.shape, master.dtype),
-            pltpu.HBM(momentum.shape, momentum.dtype),
-            pltpu.HBM((paths, rows, out_width), jnp.bfloat16),
-        ],
+        out_shape=results,
         input_output_aliases={6 + i: i for i in range(len(earlier))},
         compiler_params=pltpu.CompilerParams(vmem_limit_bytes=small_vmem),
         cost_estimate=pl.CostEstimate(
             flops=4 * rec.size,
             bytes_accessed=6 * rec.size + 16 * slot_total * rows * width,
             transcendentals=0,
+        ),
+    )(slots, blocks, shares, rec, master, momentum, *earlier)
+
+
+def last_update_kernel(first, slots, blocks, shares, rec, master, momentum, *refs):
+    new_master, new_momentum, outgoing, fresh, moved, leaving, sent = refs[3:]
+    paths, slot_total, width = rec.shape[0], master.shape[0], rec.shape[2]
+    unit = width // 2
+    start = pl.multiple_of(blocks[0] * width, width)
+    copies = []
+    for k in range(2):
+        cut = slice(k * unit, (k + 1) * unit)
+        fresh[:, :, cut] = jnp.zeros((slot_total, rec.shape[1], unit), jnp.float32)
+        for p in range(paths):
+            fresh[slots[p], :, cut] += rec[p, :, cut]
+        for m in range(slot_total):
+            mean = fresh[m, :, cut] * shares[m]
+            moved[m, :, cut] = momentum_coef * momentum[m, :, cut] + mean
+            fresh[m, :, cut] = master[m, :, cut] - outer_rate * (
+                mean + momentum_coef * moved[m, :, cut]
+            )
+        for p in range(paths):
+            leaving[p, :, cut] = fresh[slots[p], :, cut].astype(leaving.dtype)
+        for source, target, place in (
+            (leaving, outgoing, first + k * unit),
+            (fresh, new_master, start + k * unit),
+            (moved, new_momentum, start + k * unit),
+        ):
+            here = pl.ds(pl.multiple_of(place, unit), unit)
+            copies.append(
+                pltpu.make_async_copy(
+                    source.at[:, :, cut], target.at[:, :, here], sent.at[len(copies)]
+                )
+            )
+            copies[-1].start()
+    for copy in copies:
+        copy.wait()
+
+
+def last_update(slots, blocks, shares, rec, master, momentum, earlier, first):
+    block = (master.shape[0], rec.shape[1], rec.shape[2])
+    number, inside = (pl.BlockSpec(memory_space=m) for m in (pltpu.SMEM, pltpu.VMEM))
+    whole = pl.BlockSpec(memory_space=pl.ANY)
+    rec, master, momentum = [
+        pltpu.with_memory_space_constraint(x, pltpu.VMEM) for x in (rec, master, momentum)
+    ]
+    earlier = [pltpu.with_memory_space_constraint(x, pltpu.HBM) for x in earlier]
+    return pl.pallas_call(
+        functools.partial(last_update_kernel, first),
+        in_specs=[number] * 3 + [inside] * 3 + [whole] * 3,
+        out_specs=[whole] * 3,
+        out_shape=[pltpu.HBM(x.shape, x.dtype) for x in earlier],
+        scratch_shapes=[
+            pltpu.VMEM(block, jnp.float32),
+            pltpu.VMEM(block, jnp.float32),
+            pltpu.VMEM(rec.shape, jnp.bfloat16),
+            pltpu.SemaphoreType.DMA((6,)),
+        ],
+        input_output_aliases={6 + i: i for i in range(3)},
+        compiler_params=pltpu.CompilerParams(vmem_limit_bytes=small_vmem),
+        cost_estimate=pl.CostEstimate(
+            flops=4 * rec.size, bytes_accessed=8 * rec.size, transcendentals=0
         ),
     )(slots, blocks, shares, rec, master, momentum, *earlier)
 
@@ -86,6 +151,7 @@
 def place(orders, which, pieces):
     rows, width = pieces[0].shape
     whole = len(orders[0]) * width
+    pieces = [pltpu.with_memory_space_constraint(piece, pltpu.HBM) for piece in pieces]
     tile = rows // 2
     return pl.pallas_call(
         functools.partial(place_kernel, orders),
@@ -176,49 +242,65 @@
     drift = inner_drift[0]
     turned_inputs = lax.optimization_barrier(inputs.T)
 
-    def pseudo_pieces(block, first):
-        columns = block.shape[1]
+    def drift_columns(block):
+        return lax.dynamic_slice(drift, (0, block * width), (drift.shape[0], width))
+
+    def pseudo_pieces(block, moved):
         raw = jnp.dot(turned_inputs, block, preferred_element_type=jnp.float32)
-        moved = lax.dynamic_slice(drift, (0, first), (drift.shape[0], columns))
         value = (moved + inner_rate * (raw * unit_scale)) * pseudo_lift
-        return value.astype(jnp.float16).reshape(paths, rows, columns)
-
-    def exchange(parts):
-        whole = parts[0] if len(parts) == 1 else jnp.concatenate(parts, axis=2)
-        return lax.all_to_all(whole, "path", split_axis=0, concat_axis=0, tiled=True)
-
-    def updated(got, blocks, earlier, out_width, first=0):
-        rec = got.astype(jnp.float32) * (1.0 / pseudo_lift)
+        return value.astype(jnp.float16).reshape(paths, rows, width)
+
+    def exchange(pieces):
+        return lax.all_to_all(pieces, "path", split_axis=0, concat_axis=0, tiled=True)
+
+    def received(got):
+        return got.astype(jnp.float32) * (1.0 / pseudo_lift)
+
+    def updated(rec, blocks, earlier, **choice):
         order = jnp.stack(blocks).astype(jnp.int32)
-        return update(slots, order, shares, rec, master, momentum, earlier, out_width, first)
+        return update(slots, order, shares, rec, master, momentum, earlier, **choice)
 
     first_block = stepped(out_grad, 1)
-    second_block = stepped(out_grad, -1)
-    got = exchange([pseudo_pieces(out_grad, here * width)])
-    *earlier, outgoing = updated(got, [here], [], width)
-    own_sent = exchange([outgoing]).reshape(paths * rows, width)
-    first_block, second_block, own_sent = lax.optimization_barrier(
-        (first_block, second_block, own_sent)
-    )
+    pieces = pseudo_pieces(out_grad, drift_columns(here))
+    pieces, late_grad = lax.optimization_barrier((pieces, out_grad))
+    second_block = stepped(late_grad, -1)
+    got = exchange(pieces)
+    *earlier, outgoing = updated(received(got), [here], [], out_width=width)
+    own_sent = exchange(outgoing).reshape(paths * rows, width)
+    first, second = jnp.where(odd == 0, left, right), jnp.where(odd == 0, right, left)
+    far_store = [
+        lax.dynamic_slice(store, (0, 0, far * width), (slot_total, rows, width))
+        for store in (master, momentum)
+    ]
+    first_block, own_sent, far_store = lax.optimization_barrier((first_block, own_sent, far_store))
+    first_pieces = pseudo_pieces(first_block, drift_columns(first))
+    first_block, first_pieces = lax.optimization_barrier((first_block, first_pieces))
     far_block = stepped(first_block, 1)
 
-    first, second = jnp.where(odd == 0, left, right), jnp.where(odd == 0, right, left)
-    got = exchange(
-        [pseudo_pieces(first_block, first * width), pseudo_pieces(second_block, second * width)]
-    )
-    far_pieces = pseudo_pieces(far_block, far * width)
+    second_pieces = pseudo_pieces(second_block, drift_columns(second))
+    got = exchange(jnp.concatenate([first_pieces, second_pieces], axis=2))
+    far_pieces = pseudo_pieces(far_block, drift_columns(far))
     got, far_pieces = lax.optimization_barrier((got, far_pieces))
-    far_got = exchange([far_pieces])
+    far_got = exchange(far_pieces)
     even_path = (jnp.arange(paths) % 2 == 0)[:, None, None]
     left_got = jnp.where(even_path, got[:, :, :width], got[:, :, width:])
     right_got = jnp.where(even_path, got[:, :, width:], got[:, :, :width])
     *earlier, outgoing = updated(
-        jnp.concatenate([left_got, right_got], axis=2), [left, right], earlier, 3 * width
-    )
-    new_master, new_momentum, outgoing = updated(
-        far_got, [far], [*earlier, outgoing], 3 * width, 2 * width
-    )
-    sent = exchange([outgoing]).reshape(paths * rows, 3 * width)
+        received(jnp.concatenate([left_got, right_got], axis=2)),
+        [left, right],
+        earlier,
+        out_width=3 * width,
+    )
+    new_master, new_momentum, outgoing = last_update(
+        slots,
+        far.astype(jnp.int32)[None],
+        shares,
+        received(far_got),
+        *far_store,
+        [*earlier, outgoing],
+        2 * width,
+    )
+    sent = exchange(outgoing).reshape(paths * rows, 3 * width)
 
     blocks = [out_grad, first_block, second_block, far_block]
     starts = jnp.stack([here, first, second, far]).astype(jnp.int32) * width

time: 136 us -> 134 us (0.985)
  blocking collectives: 15.6 us -> 0 us
  waiting for transfers between devices: 40.6 us -> 47.2 us
  starting transfers between devices: 31.5 us -> 35.7 us
    all_to_all x1 -> x0, blocking collectives: 15.6 us -> none  [exchange(): lax.all_to_all(whole, 'path', split_axis=0, concat_axis=0, tiled=True)]
    all_to_all x4 -> x5, waiting for transfers between devices: 28.1 us -> 33 us  [exchange(): lax.all_to_all(pieces, 'path', split_axis=0, concat_axis=0, tiled=True)]
    all_to_all x4 -> x5, starting transfers between devices: 26.3 us -> 30.6 us  [exchange(): lax.all_to_all(pieces, 'path', split_axis=0, concat_axis=0, tiled=True)]
    ppermute x3, waiting for transfers between devices: 12.5 us -> 14.2 us  [stepped(): lax.ppermute(block, ('path', 'shard'), [(p * size + y, p * size + (y + (s...]
    unnamed x11 -> x13, local copies, waits for them, and re-layouts: 7.13 us -> 7.13 us
  transfers between devices with their start and end apart: 7 -> 8, of which waited for: 6 -> 5; matrix products, arithmetic and copies ran while one was open for 16% -> 18% of each run, Pallas kernels for 12% -> 12%
where the time goes in v4:
time: 134 us; the launch traced here: 133 us
  waiting for transfers between devices  47.2 us (35%)
  starting transfers between devices  35.7 us (27%)
  Pallas kernels  20.8 us (16%)
  matrix products  15.2 us (11%)
  local copies, waits for them, and re-layouts  8.41 us (6%)
  other arithmetic  4.76 us (4%)
    all_to_all x5, waiting for transfers between devices, exchange(): lax.all_to_all(pieces, 'path', split_axis=0, concat_axis=0, tiled=True)  33 us
    all_to_all x5, starting transfers between devices, exchange(): lax.all_to_all(pieces, 'path', split_axis=0, concat_axis=0, tiled=True)  30.6 us
    dot_general x4, matrix products, pseudo_pieces(): raw = jnp.dot(turned_inputs, block, preferred_element_type=jnp.float32)  15.2 us
    ppermute x3, waiting for transfers between devices, stepped(): lax.ppermute(block, ('path', 'shard'), [(p * size + y, p * size + (y + (s...  14.2 us
    pallas_call x1, Pallas kernels, input_gradient(): pl.pallas_call(functools.partial(back_kernel, scale), grid_spec=pltpu.Pre...  8.1 us
    pallas_call x2, Pallas kernels, update(): pl.pallas_call(functools.partial(update_kernel, stores, out_width > 0), g...  7.98 us
    unnamed x13, local copies, waits for them, and re-layouts  7.13 us
    ppermute x3, starting transfers between devices, stepped(): lax.ppermute(block, ('path', 'shard'), [(p * size + y, p * size + (y + (s...  5.14 us
  transfers between devices with their start and end apart: 8, of which 5 were waited for; matrix products, arithmetic and copies ran while one was open for 18% of the time, Pallas kernels for 12%

profile of v4, /device:TPU:0, one launch (start us, length us, event | category | flops | bytes accessed | tf_op | source)
XLA Modules:
  0.0 132.8 jit_solution(6513094160057843596)
XLA Ops:
  0.6 0.0 copy-start
  0.6 1.7 %collective-permute-start = (bf16[2048,512]{1,0:T(8,128)(2,1)}, bf16[2048,512]{1,0:T(8,128)(2,1)}, u32[]{:S(2)}, u32[]{:S(2)}) collective-permute-start(bf16[2048,512]{1,0:T(8,128)(2,1)} %refs_0_.1), channel_id=1, source_target_pairs={{0,1},{1,2},{2,3},{3,0},{4,7},{5,4},{6,5},{7,6},{8,9},{9,10},{10,1... | collective-permute-start | bytes 6291464 | tf_op jit(solution)/shard_map/ppermute | solution.py:224
  2.4 0.0 copy-done
  2.4 0.0 copy-start.4
  2.4 0.0 copy-start.5
  2.4 4.0 %fusion.14 = f16[512,512]{1,0:T(8,128)(2,1)} fusion(bf16[512,2048]{0,1:T(8,128)(2,1)S(1)} %bitcast.59, bf16[2048,512]{1,0:T(8,128)(2,1)} %refs_0_.1, f32[1,512,2048]{2,1,0:T(8,128)} %param.11, s32[]{:T(128)S(6)} %select_n.64), kind=kOutput, calls=%fused_computation.19 | convolution fusion | flops 1074790400 | bytes 5767172 | tf_op jit(solution)/shard_map/dot_general | solution.py:249
  6.4 8.8 %all-to-all-start = ((f16[32,16,512]{2,1,0:T(8,128)(2,1)}), f16[32,16,512]{2,1,0:T(8,128)(2,1)S(1)}, u32[]{:S(2)}, u32[]{:S(2)}) async-start(f16[32,16,512]{2,1,0:T(8,128)(2,1)} %bitcast.5), calls=%async_computation | async-start | bytes 1048576 | tf_op jit(solution)/shard_map/all_to_all | solution.py:254
  15.1 2.4 %collective-permute-start.1 = (bf16[2048,512]{1,0:T(8,128)(2,1)}, bf16[2048,512]{1,0:T(8,128)(2,1)}, u32[]{:S(2)}, u32[]{:S(2)}) collective-permute-start(bf16[2048,512]{1,0:T(8,128)(2,1)} %refs_0_.1), channel_id=1, source_target_pairs={{0,3},{1,0},{2,1},{3,2},{4,5},{5,6},{6,7},{7,4},{8,11},{9,8},{10,9... | collective-permute-start | bytes 6291464 | tf_op jit(solution)/shard_map/ppermute | solution.py:224
  17.5 0.0 copy-done.4
  17.6 0.0 copy-done.5
  17.6 0.1 select_reduce_fusion.slots
  17.6 0.1 convert_reduce_fusion
  17.8 9.1 %all-to-all-done = f16[32,16,512]{2,1,0:T(8,128)(2,1)S(1)} async-done(((f16[32,16,512]{2,1,0:T(8,128)(2,1)}), f16[32,16,512]{2,1,0:T(8,128)(2,1)S(1)}, u32[]{:S(2)}, u32[]{:S(2)}) %all-to-all-start) | async-done | bytes 524320 | tf_op jit(solution)/shard_map/all_to_all | solution.py:254
  26.9 0.1 convert_multiply_fusion.2.rec
  27.0 3.0 %shard_map.111 = (f32[16,16,2048]{2,1,0:T(8,128)}, f32[16,16,2048]{2,1,0:T(8,128)}, bf16[32,16,512]{2,1,0:T(8,128)(2,1)}) custom-call(s32[32]{0:T(128)S(1)} %select_reduce_fusion.slots, s32[1]{0:T(128)} %bitcast.2.blocks.which, f32[16]{0:T(128)S(1)} %broadcast_divide_fusion.shares, f32[32,16,512]{2,1,0:T(8,128)S(1)} %convert_multiply_fusion.2.rec, ...), custom_call_target="tpu_custom_call" | custom-call | flops 1048576 | bytes 3670016 | tf_op jit(solution)/shard_map/pallas_call | solution.py:54
  30.0 4.6 %all-to-all-start.1 = ((bf16[32,16,512]{2,1,0:T(8,128)(2,1)}), bf16[32,16,512]{2,1,0:T(8,128)(2,1)}, u32[]{:S(2)}, u32[]{:S(2)}) async-start(bf16[32,16,512]{2,1,0:T(8,128)(2,1)} %get-tuple-element.28), calls=%async_computation.1 | async-start | bytes 1048576 | tf_op jit(solution)/shard_map/all_to_all | solution.py:254
  34.7 1.3 constant_dynamic-slice_fusion
  36.0 10.4 %all-to-all-done.1 = bf16[32,16,512]{2,1,0:T(8,128)(2,1)} async-done(((bf16[32,16,512]{2,1,0:T(8,128)(2,1)}), bf16[32,16,512]{2,1,0:T(8,128)(2,1)}, u32[]{:S(2)}, u32[]{:S(2)}) %all-to-all-start.1) | async-done | bytes 524320 | tf_op jit(solution)/shard_map/all_to_all | solution.py:254
  46.4 0.0 collective-permute-done.refs_1_
  46.4 4.0 %fusion.13 = f16[512,512]{1,0:T(8,128)(2,1)} fusion(bf16[2048,512]{1,0:T(8,128)(2,1)} %collective-permute-done.refs_1_, bf16[512,2048]{0,1:T(8,128)(2,1)S(1)} %bitcast.60, f32[1,512,2048]{2,1,0:T(8,128)} %param.11, s32[]{:T(128)S(6)} %select_n.70), kind=kOutput, calls=%fused_computation.18 | convolution fusion | flops 1074790400 | bytes 5767172 | tf_op jit(solution)/shard_map/dot_general | solution.py:249
  50.4 1.0 collective-permute-start.2
  51.4 0.0 copy-start.3
  51.4 0.0 collective-permute-done.1.refs_2_
  51.4 3.2 %fusion.12 = f16[512,512]{1,0:T(8,128)(2,1)S(1)} fusion(bf16[2048,512]{1,0:T(8,128)(2,1)} %collective-permute-done.1.refs_2_, bf16[512,2048]{0,1:T(8,128)(2,1)S(1)} %bitcast.61, f32[1,512,2048]{2,1,0:T(8,128)} %param.11, s32[]{:T(128)S(6)} %select_n.72), kind=kOutput, calls=%fused_computation.17 | convolution fusion | flops 1074790400 | bytes 5767172 | tf_op jit(solution)/shard_map/dot_general | solution.py:249
  54.6 0.0 copy-done.3
  54.6 1.2 pad_maximum_fusion
  55.9 7.8 %all-to-all-start.2 = ((f16[32,16,1024]{2,1,0:T(8,128)(2,1)}), f16[32,16,1024]{2,1,0:T(8,128)(2,1)}, u32[]{:S(2)}, u32[]{:S(2)}) async-start(f16[32,16,1024]{2,1,0:T(8,128)(2,1)} %pad_maximum_fusion), calls=%async_computation.2 | async-start | bytes 2097152 | tf_op jit(solution)/shard_map/all_to_all | solution.py:254
  63.7 14.2 %collective-permute-done.2.refs_3_ = bf16[2048,512]{1,0:T(8,128)(2,1)} collective-permute-done((bf16[2048,512]{1,0:T(8,128)(2,1)}, bf16[2048,512]{1,0:T(8,128)(2,1)}, u32[]{:S(2)}, u32[]{:S(2)}) %collective-permute-start.2) | collective-permute-done | bytes 2097184 | tf_op jit(solution)/shard_map/ppermute | solution.py:224
  78.0 4.0 %fusion.11 = f16[512,512]{1,0:T(8,128)(2,1)} fusion(bf16[2048,512]{1,0:T(8,128)(2,1)} %collective-permute-done.2.refs_3_, bf16[512,2048]{0,1:T(8,128)(2,1)S(1)} %bitcast.58, f32[1,512,2048]{2,1,0:T(8,128)} %param.11, s32[]{:T(128)S(6)} %select_n.65), kind=kOutput, calls=%fused_computation.16 | convolution fusion | flops 1074790400 | bytes 5767172 | tf_op jit(solution)/shard_map/dot_general | solution.py:249
  81.9 0.0 all-to-all-done.2
  81.9 4.6 %all-to-all-start.3 = ((f16[32,16,512]{2,1,0:T(8,128)(2,1)}), f16[32,16,512]{2,1,0:T(8,128)(2,1)}, u32[]{:S(2)}, u32[]{:S(2)}) async-start(f16[32,16,512]{2,1,0:T(8,128)(2,1)} %bitcast.64), calls=%async_computation.3 | async-start | bytes 1048576 | tf_op jit(solution)/shard_map/all_to_all | solution.py:254
  86.6 0.1 pad_add_fusion.blocks
  86.6 1.5 %broadcast_select_fusion.1 = (f16[32,16,512]{2,1,0:T(8,128)(2,1)S(1)}, f16[32,16,512]{2,1,0:T(8,128)(2,1)S(1)}) fusion(pred[32]{0:T(512)(128)(4,1)S(1)} %fusion.15, f16[32,16,1024]{2,1,0:T(8,128)(2,1)} %all-to-all-done.2), kind=kLoop, calls=%fused_computation.24 | loop fusion | flops 524288 | bytes 2097184 | tf_op jit(solution)/shard_map/jit(_where)/select_n | solution.py:286
  88.2 0.3 convert_multiply_fusion.rec
  88.5 5.0 %shard_map.112 = (f32[16,16,2048]{2,1,0:T(8,128)}, f32[16,16,2048]{2,1,0:T(8,128)}, bf16[32,16,1536]{2,1,0:T(8,128)(2,1)}) custom-call(s32[32]{0:T(128)S(1)} %select_reduce_fusion.slots, s32[2]{0:T(128)S(1)} %pad_add_fusion.blocks, f32[16]{0:T(128)S(1)} %broadcast_divide_fusion.shares, ...), custom_call_target="tpu_custom_call", output_to_operand_aliasing={{0}: (6, {}), {1}: (7, {})} | custom-call | flops 2097152 | bytes 7340032 | tf_op jit(solution)/shard_map/pallas_call | solution.py:54
  93.5 4.8 %all-to-all-done.3 = f16[32,16,512]{2,1,0:T(8,128)(2,1)} async-done(((f16[32,16,512]{2,1,0:T(8,128)(2,1)}), f16[32,16,512]{2,1,0:T(8,128)(2,1)}, u32[]{:S(2)}, u32[]{:S(2)}) %all-to-all-start.3) | async-done | bytes 524320 | tf_op jit(solution)/shard_map/all_to_all | solution.py:254
  98.3 1.2 convert_multiply_fusion.1.rec
  99.5 2.0 %shard_map.113 = (f32[16,16,2048]{2,1,0:T(8,128)}, f32[16,16,2048]{2,1,0:T(8,128)}, bf16[32,16,1536]{2,1,0:T(8,128)(2,1)}) custom-call(s32[32]{0:T(128)S(1)} %select_reduce_fusion.slots, s32[1]{0:T(128)} %bitcast.1.blocks, f32[16]{0:T(128)S(1)} %broadcast_divide_fusion.shares, ...), custom_call_target="tpu_custom_call", output_to_operand_aliasing={{0}: (6, {}), {1}: (7, {}), {2}: (8, {})} | custom-call | flops 1048576 | bytes 2097152 | tf_op jit(solution)/shard_map/pallas_call | solution.py:117
  101.5 4.7 %all-to-all-start.4 = ((bf16[32,16,1536]{2,1,0:T(8,128)(2,1)}), bf16[32,16,1536]{2,1,0:T(8,128)(2,1)}, u32[]{:S(2)}, u32[]{:S(2)}) async-start(bf16[32,16,1536]{2,1,0:T(8,128)(2,1)} %get-tuple-element.42), calls=%async_computation.4 | async-start | bytes 3145728 | tf_op jit(solution)/shard_map/all_to_all | solution.py:254
  106.3 3.9 %copy.20 = bf16[1,512,2048]{1,2,0:T(8,128)(2,1)} copy(bf16[1,512,2048]{2,1,0:T(8,128)(2,1)} %param.10) | data formatting | bytes 4194304 | tf_op args[2]
  110.2 0.1 add_multiply_fusion.starts
  110.3 0.0 copy-start.1
  110.3 1.6 %copy-done.1 = bf16[2048,512]{1,0:T(8,128)(2,1)S(1)} copy-done((bf16[2048,512]{1,0:T(8,128)(2,1)S(1)}, bf16[2048,512]{1,0:T(8,128)(2,1)}, u32[]{:S(2)}) %copy-start.1) | copy-done | bytes 2097176
  111.9 0.0 copy-start.2
  111.9 1.6 %copy-done.2 = bf16[1,512,2048]{1,2,0:T(8,128)(2,1)S(1)} copy-done((bf16[1,512,2048]{1,2,0:T(8,128)(2,1)S(1)}, bf16[1,512,2048]{1,2,0:T(8,128)(2,1)}, u32[]{:S(2)}) %copy-start.2) | copy-done | bytes 2097176
  113.5 8.1 %shard_map.114 = bf16[2048,512]{1,0:T(8,128)(2,1)} custom-call(s32[4]{0:T(128)S(1)} %add_multiply_fusion.starts, bf16[2048,512]{1,0:T(8,128)(2,1)S(1)} %bitcast.62, bf16[2048,512]{1,0:T(8,128)(2,1)S(1)} %copy-done.1, bf16[2048,512]{1,0:T(8,128)(2,1)} %collective-permute-done.refs_1_, bf16[2048,512]{1,0:T(8,128)(2,1)} %collective-permute-done.1.refs_2_, ...), custom_call_target="tpu_custom_call" | custom-call | flops 4294967296 | bytes 12582912 | tf_op jit(solution)/shard_map/pallas_call | solution.py:188
  121.6 8.6 %all-to-all-done.4 = bf16[32,16,1536]{2,1,0:T(8,128)(2,1)} async-done(((bf16[32,16,1536]{2,1,0:T(8,128)(2,1)}), bf16[32,16,1536]{2,1,0:T(8,128)(2,1)}, u32[]{:S(2)}, u32[]{:S(2)}) %all-to-all-start.4) | async-done | bytes 1572896 | tf_op jit(solution)/shard_map/all_to_all | solution.py:254
  130.2 2.6 %shard_map.115 = bf16[512,2048]{1,0:T(8,128)(2,1)} custom-call(s32[1]{0:T(128)} %bitcast.2.blocks.which, bf16[512,512]{1,0:T(8,128)(2,1)} %bitcast.6.refs_0_, bf16[512,1536]{1,0:T(8,128)(2,1)} %bitcast.18.refs_1_), custom_call_target="tpu_custom_call" | custom-call | bytes 4194304 | tf_op jit(solution)/shard_map/pallas_call | solution.py:156
  (2 shorter events, 0.0 us)
Async XLA Ops:
  0.6 1.7 %copy-start = (bf16[2048,512]{1,0:T(8,128)(2,1)S(1)}, bf16[2048,512]{1,0:T(8,128)(2,1)}, u32[]{:S(2)}) copy-start(bf16[2048,512]{1,0:T(8,128)(2,1)} %param.8) | copy-start | bytes 6291460
  0.6 45.8 %collective-permute-start = (bf16[2048,512]{1,0:T(8,128)(2,1)}, bf16[2048,512]{1,0:T(8,128)(2,1)}, u32[]{:S(2)}, u32[]{:S(2)}) collective-permute-start(bf16[2048,512]{1,0:T(8,128)(2,1)} %refs_0_.1), channel_id=1, source_target_pairs={{0,1},{1,2},{2,3},{3,0},{4,7},{5,4},{6,5},{7,6},{8,9},{9,10},{10,1... | collective-permute-start | bytes 6291464 | tf_op jit(solution)/shard_map/ppermute | solution.py:224
  2.4 15.2 %copy-start.4 = (s32[16]{0:T(128)S(1)}, s32[16]{0:T(128)}, u32[]{:S(2)}) copy-start(s32[16]{0:T(128)} %param.13) | copy-start | bytes 196
  2.4 15.2 %copy-start.5 = (s32[32,1]{0,1:T(1,128)S(1)}, s32[32,1]{0,1:T(1,128)}, u32[]{:S(2)}) copy-start(s32[32,1]{0,1:T(1,128)} %param.12) | copy-start | bytes 388
  6.4 20.5 %all-to-all-start = ((f16[32,16,512]{2,1,0:T(8,128)(2,1)}), f16[32,16,512]{2,1,0:T(8,128)(2,1)S(1)}, u32[]{:S(2)}, u32[]{:S(2)}) async-start(f16[32,16,512]{2,1,0:T(8,128)(2,1)} %bitcast.5), calls=%async_computation | async-start | bytes 1048576 | tf_op jit(solution)/shard_map/all_to_all | solution.py:254
  15.1 36.3 %collective-permute-start.1 = (bf16[2048,512]{1,0:T(8,128)(2,1)}, bf16[2048,512]{1,0:T(8,128)(2,1)}, u32[]{:S(2)}, u32[]{:S(2)}) collective-permute-start(bf16[2048,512]{1,0:T(8,128)(2,1)} %refs_0_.1), channel_id=1, source_target_pairs={{0,3},{1,0},{2,1},{3,2},{4,5},{5,6},{6,7},{7,4},{8,11},{9,8},{10,9... | collective-permute-start | bytes 6291464 | tf_op jit(solution)/shard_map/ppermute | solution.py:224
  30.0 16.4 %all-to-all-start.1 = ((bf16[32,16,512]{2,1,0:T(8,128)(2,1)}), bf16[32,16,512]{2,1,0:T(8,128)(2,1)}, u32[]{:S(2)}, u32[]{:S(2)}) async-start(bf16[32,16,512]{2,1,0:T(8,128)(2,1)} %get-tuple-element.28), calls=%async_computation.1 | async-start | bytes 1048576 | tf_op jit(solution)/shard_map/all_to_all | solution.py:254
  50.4 27.6 %collective-permute-start.2 = (bf16[2048,512]{1,0:T(8,128)(2,1)}, bf16[2048,512]{1,0:T(8,128)(2,1)}, u32[]{:S(2)}, u32[]{:S(2)}) collective-permute-start(bf16[2048,512]{1,0:T(8,128)(2,1)} %collective-permute-done.refs_1_), channel_id=1, source_target_pairs={{0,1},{1,2},{2,3},{3,0},{4,7},{5,4},{6,5},{7,6},{8,9},{9,10},{10,1... | collective-permute-start | bytes 6291464 | tf_op jit(solution)/shard_map/ppermute | solution.py:224
  51.4 3.3 %copy-start.3 = (f16[512,512]{1,0:T(8,128)(2,1)S(1)}, f16[512,512]{1,0:T(8,128)(2,1)}, u32[]{:S(2)}) copy-start(f16[512,512]{1,0:T(8,128)(2,1)} %fusion.13) | copy-start | bytes 1572868
  55.9 26.1 %all-to-all-start.2 = ((f16[32,16,1024]{2,1,0:T(8,128)(2,1)}), f16[32,16,1024]{2,1,0:T(8,128)(2,1)}, u32[]{:S(2)}, u32[]{:S(2)}) async-start(f16[32,16,1024]{2,1,0:T(8,128)(2,1)} %pad_maximum_fusion), calls=%async_computation.2 | async-start | bytes 2097152 | tf_op jit(solution)/shard_map/all_to_all | solution.py:254
  81.9 16.4 %all-to-all-start.3 = ((f16[32,16,512]{2,1,0:T(8,128)(2,1)}), f16[32,16,512]{2,1,0:T(8,128)(2,1)}, u32[]{:S(2)}, u32[]{:S(2)}) async-start(f16[32,16,512]{2,1,0:T(8,128)(2,1)} %bitcast.64), calls=%async_computation.3 | async-start | bytes 1048576 | tf_op jit(solution)/shard_map/all_to_all | solution.py:254
  101.5 28.6 %all-to-all-start.4 = ((bf16[32,16,1536]{2,1,0:T(8,128)(2,1)}), bf16[32,16,1536]{2,1,0:T(8,128)(2,1)}, u32[]{:S(2)}, u32[]{:S(2)}) async-start(bf16[32,16,1536]{2,1,0:T(8,128)(2,1)} %get-tuple-element.42), calls=%async_computation.4 | async-start | bytes 3145728 | tf_op jit(solution)/shard_map/all_to_all | solution.py:254
  110.3 1.6 %copy-start.1 = (bf16[2048,512]{1,0:T(8,128)(2,1)S(1)}, bf16[2048,512]{1,0:T(8,128)(2,1)}, u32[]{:S(2)}) copy-start(bf16[2048,512]{1,0:T(8,128)(2,1)} %refs_0_.1) | copy-start | bytes 6291460
  111.9 1.6 %copy-start.2 = (bf16[1,512,2048]{1,2,0:T(8,128)(2,1)S(1)}, bf16[1,512,2048]{1,2,0:T(8,128)(2,1)}, u32[]{:S(2)}) copy-start(bf16[1,512,2048]{1,2,0:T(8,128)(2,1)} %copy.20) | copy-start | bytes 6291460

commit v5 on v4

--- a/solution.py
+++ b/solution.py
@@ -151,7 +151,6 @@
 def place(orders, which, pieces):
     rows, width = pieces[0].shape
     whole = len(orders[0]) * width
-    pieces = [pltpu.with_memory_space_constraint(piece, pltpu.HBM) for piece in pieces]
     tile = rows // 2
     return pl.pallas_call(
         functools.partial(place_kernel, orders),
@@ -275,10 +274,11 @@
     first_block, own_sent, far_store = lax.optimization_barrier((first_block, own_sent, far_store))
     first_pieces = pseudo_pieces(first_block, drift_columns(first))
     first_block, first_pieces = lax.optimization_barrier((first_block, first_pieces))
+    both_pieces = lax.optimization_barrier(jnp.pad(first_pieces, ((0, 0), (0, 0), (0, width))))
     far_block = stepped(first_block, 1)
 
     second_pieces = pseudo_pieces(second_block, drift_columns(second))
-    got = exchange(jnp.concatenate([first_pieces, second_pieces], axis=2))
+    got = exchange(lax.dynamic_update_slice(both_pieces, second_pieces, (0, 0, width)))
     far_pieces = pseudo_pieces(far_block, drift_columns(far))
     got, far_pieces = lax.optimization_barrier((got, far_pieces))
     far_got = exchange(far_pieces)

time: 134 us -> 134 us (level)
  local copies, waits for them, and re-layouts: 8.41 us -> 11.5 us
  starting transfers between devices: 35.7 us -> 33.5 us
    pad x0 -> x1, local copies, waits for them, and re-layouts: none -> 2.18 us  [on_device(): jnp.pad(first_pieces, ((0, 0), (0, 0), (0, width)))]
    all_to_all x5, starting transfers between devices: 30.6 us -> 28.4 us  [exchange(): lax.all_to_all(pieces, 'path', split_axis=0, concat_axis=0, tiled=True)]
    unnamed x13 -> x11, local copies, waits for them, and re-layouts: 7.13 us -> 7.13 us
  transfers between devices with their start and end apart: 8 -> 8, of which waited for: 5 -> 5; matrix products, arithmetic and copies ran while one was open for 18% -> 19% of each run, Pallas kernels for 12% -> 12%
where the time goes in v5:
time: 134 us; the launch traced here: 133 us
  waiting for transfers between devices  47.5 us (35%)
  starting transfers between devices  33.5 us (25%)
  Pallas kernels  20.8 us (16%)
  matrix products  15.1 us (11%)
  local copies, waits for them, and re-layouts  11.5 us (9%)
  other arithmetic  3.53 us (3%)
    all_to_all x5, waiting for transfers between devices, exchange(): lax.all_to_all(pieces, 'path', split_axis=0, concat_axis=0, tiled=True)  33 us
    all_to_all x5, starting transfers between devices, exchange(): lax.all_to_all(pieces, 'path', split_axis=0, concat_axis=0, tiled=True)  28.4 us
    dot_general x4, matrix products, pseudo_pieces(): raw = jnp.dot(turned_inputs, block, preferred_element_type=jnp.float32)  15.1 us
    ppermute x3, waiting for transfers between devices, stepped(): lax.ppermute(block, ('path', 'shard'), [(p * size + y, p * size + (y + (s...  14.6 us
    pallas_call x1, Pallas kernels, input_gradient(): pl.pallas_call(functools.partial(back_kernel, scale), grid_spec=pltpu.Pre...  8.1 us
    pallas_call x2, Pallas kernels, update(): pl.pallas_call(functools.partial(update_kernel, stores, out_width > 0), g...  8.01 us
    unnamed x11, local copies, waits for them, and re-layouts  7.13 us
    ppermute x3, starting transfers between devices, stepped(): lax.ppermute(block, ('path', 'shard'), [(p * size + y, p * size + (y + (s...  5.14 us
  transfers between devices with their start and end apart: 8, of which 5 were waited for; matrix products, arithmetic and copies ran while one was open for 19% of the time, Pallas kernels for 12%

profile of v5, /device:TPU:0, one launch (start us, length us, event | category | flops | bytes accessed | tf_op | source)
XLA Modules:
  0.0 132.8 jit_solution(6545347138587132229)
XLA Ops:
  0.6 0.0 copy-start
  0.6 1.7 %collective-permute-start = (bf16[2048,512]{1,0:T(8,128)(2,1)}, bf16[2048,512]{1,0:T(8,128)(2,1)}, u32[]{:S(2)}, u32[]{:S(2)}) collective-permute-start(bf16[2048,512]{1,0:T(8,128)(2,1)} %refs_0_.1), channel_id=1, source_target_pairs={{0,1},{1,2},{2,3},{3,0},{4,7},{5,4},{6,5},{7,6},{8,9},{9,10},{10,1... | collective-permute-start | bytes 6291464 | tf_op jit(solution)/shard_map/ppermute | solution.py:223
  2.4 0.0 copy-done
  2.4 0.0 copy-start.3
  2.4 0.0 copy-start.4
  2.4 4.0 %fusion.14 = f16[512,512]{1,0:T(8,128)(2,1)} fusion(bf16[512,2048]{0,1:T(8,128)(2,1)S(1)} %bitcast.59, bf16[2048,512]{1,0:T(8,128)(2,1)} %refs_0_.1, f32[1,512,2048]{2,1,0:T(8,128)} %param.11, s32[]{:T(128)S(6)} %select_n.64), kind=kOutput, calls=%fused_computation.19 | convolution fusion | flops 1074790400 | bytes 5767172 | tf_op jit(solution)/shard_map/dot_general | solution.py:248
  6.4 8.8 %all-to-all-start = ((f16[32,16,512]{2,1,0:T(8,128)(2,1)}), f16[32,16,512]{2,1,0:T(8,128)(2,1)S(1)}, u32[]{:S(2)}, u32[]{:S(2)}) async-start(f16[32,16,512]{2,1,0:T(8,128)(2,1)} %bitcast.5), calls=%async_computation | async-start | bytes 1048576 | tf_op jit(solution)/shard_map/all_to_all | solution.py:253
  15.1 2.4 %collective-permute-start.1 = (bf16[2048,512]{1,0:T(8,128)(2,1)}, bf16[2048,512]{1,0:T(8,128)(2,1)}, u32[]{:S(2)}, u32[]{:S(2)}) collective-permute-start(bf16[2048,512]{1,0:T(8,128)(2,1)} %refs_0_.1), channel_id=1, source_target_pairs={{0,3},{1,0},{2,1},{3,2},{4,5},{5,6},{6,7},{7,4},{8,11},{9,8},{10,9... | collective-permute-start | bytes 6291464 | tf_op jit(solution)/shard_map/ppermute | solution.py:223
  17.5 0.0 copy-done.3
  17.6 0.0 copy-done.4
  17.6 0.1 select_reduce_fusion.slots
  17.6 0.1 convert_reduce_fusion
  17.8 9.1 %all-to-all-done = f16[32,16,512]{2,1,0:T(8,128)(2,1)S(1)} async-done(((f16[32,16,512]{2,1,0:T(8,128)(2,1)}), f16[32,16,512]{2,1,0:T(8,128)(2,1)S(1)}, u32[]{:S(2)}, u32[]{:S(2)}) %all-to-all-start) | async-done | bytes 524320 | tf_op jit(solution)/shard_map/all_to_all | solution.py:253
  26.9 0.1 convert_multiply_fusion.2.rec
  27.0 3.0 %shard_map.111 = (f32[16,16,2048]{2,1,0:T(8,128)}, f32[16,16,2048]{2,1,0:T(8,128)}, bf16[32,16,512]{2,1,0:T(8,128)(2,1)}) custom-call(s32[32]{0:T(128)S(1)} %select_reduce_fusion.slots, s32[1]{0:T(128)} %bitcast.2.blocks.which, f32[16]{0:T(128)S(1)} %broadcast_divide_fusion.shares, f32[32,16,512]{2,1,0:T(8,128)S(1)} %convert_multiply_fusion.2.rec, ...), custom_call_target="tpu_custom_call" | custom-call | flops 1048576 | bytes 3670016 | tf_op jit(solution)/shard_map/pallas_call | solution.py:54
  30.0 4.6 %all-to-all-start.1 = ((bf16[32,16,512]{2,1,0:T(8,128)(2,1)}), bf16[32,16,512]{2,1,0:T(8,128)(2,1)}, u32[]{:S(2)}, u32[]{:S(2)}) async-start(bf16[32,16,512]{2,1,0:T(8,128)(2,1)} %get-tuple-element.28), calls=%async_computation.1 | async-start | bytes 1048576 | tf_op jit(solution)/shard_map/all_to_all | solution.py:253
  34.7 1.3 constant_dynamic-slice_fusion
  36.0 10.4 %all-to-all-done.1 = bf16[32,16,512]{2,1,0:T(8,128)(2,1)} async-done(((bf16[32,16,512]{2,1,0:T(8,128)(2,1)}), bf16[32,16,512]{2,1,0:T(8,128)(2,1)}, u32[]{:S(2)}, u32[]{:S(2)}) %all-to-all-start.1) | async-done | bytes 524320 | tf_op jit(solution)/shard_map/all_to_all | solution.py:253
  46.4 0.0 collective-permute-done.refs_1_
  46.4 4.0 %fusion.13 = f16[512,512]{1,0:T(8,128)(2,1)} fusion(bf16[2048,512]{1,0:T(8,128)(2,1)} %collective-permute-done.refs_1_, bf16[512,2048]{0,1:T(8,128)(2,1)S(1)} %bitcast.60, f32[1,512,2048]{2,1,0:T(8,128)} %param.11, s32[]{:T(128)S(6)} %select_n.70), kind=kOutput, calls=%fused_computation.18 | convolution fusion | flops 1074790400 | bytes 5767172 | tf_op jit(solution)/shard_map/dot_general | solution.py:248
  50.4 1.0 collective-permute-start.2
  51.4 2.2 %pad.4 = f16[32,16,1024]{2,1,0:T(8,128)(2,1)} pad(f16[32,16,512]{2,1,0:T(8,128)(2,1)} %bitcast.65, f16[]{:T(256)} %constant.80.clone.1), padding=0_0x0_0x0_512 | pad | bytes 1572866 | tf_op jit(solution)/shard_map/jit(_pad)/pad | solution.py:277
  53.6 0.0 collective-permute-done.1.refs_2_
  53.6 3.2 %fusion.12 = f16[512,512]{1,0:T(8,128)(2,1)S(1)} fusion(bf16[2048,512]{1,0:T(8,128)(2,1)} %collective-permute-done.1.refs_2_, bf16[512,2048]{0,1:T(8,128)(2,1)S(1)} %bitcast.61, f32[1,512,2048]{2,1,0:T(8,128)} %param.11, s32[]{:T(128)S(6)} %select_n.72), kind=kOutput, calls=%fused_computation.17 | convolution fusion | flops 1074790400 | bytes 5767172 | tf_op jit(solution)/shard_map/dot_general | solution.py:248
  56.8 0.9 constant_dynamic-update-slice_fusion
  57.7 5.7 %all-to-all-start.2 = ((f16[32,16,1024]{2,1,0:T(8,128)(2,1)}), f16[32,16,1024]{2,1,0:T(8,128)(2,1)}, u32[]{:S(2)}, u32[]{:S(2)}) async-start(f16[32,16,1024]{2,1,0:T(8,128)(2,1)} %constant_dynamic-update-slice_fusion), calls=%async_computation.2 | async-start | bytes 2097152 | tf_op jit(solution)/shard_map/all_to_all | solution.py:253
  63.4 14.6 %collective-permute-done.2.refs_3_ = bf16[2048,512]{1,0:T(8,128)(2,1)} collective-permute-done((bf16[2048,512]{1,0:T(8,128)(2,1)}, bf16[2048,512]{1,0:T(8,128)(2,1)}, u32[]{:S(2)}, u32[]{:S(2)}) %collective-permute-start.2) | collective-permute-done | bytes 2097184 | tf_op jit(solution)/shard_map/ppermute | solution.py:223
  78.0 4.0 %fusion.11 = f16[512,512]{1,0:T(8,128)(2,1)} fusion(bf16[2048,512]{1,0:T(8,128)(2,1)} %collective-permute-done.2.refs_3_, bf16[512,2048]{0,1:T(8,128)(2,1)S(1)} %bitcast.58, f32[1,512,2048]{2,1,0:T(8,128)} %param.11, s32[]{:T(128)S(6)} %select_n.65), kind=kOutput, calls=%fused_computation.16 | convolution fusion | flops 1074790400 | bytes 5767172 | tf_op jit(solution)/shard_map/dot_general | solution.py:248
  81.9 0.0 all-to-all-done.2
  81.9 4.6 %all-to-all-start.3 = ((f16[32,16,512]{2,1,0:T(8,128)(2,1)}), f16[32,16,512]{2,1,0:T(8,128)(2,1)}, u32[]{:S(2)}, u32[]{:S(2)}) async-start(f16[32,16,512]{2,1,0:T(8,128)(2,1)} %bitcast.64), calls=%async_computation.3 | async-start | bytes 1048576 | tf_op jit(solution)/shard_map/all_to_all | solution.py:253
  86.6 0.1 pad_add_fusion.blocks
  86.6 1.5 %broadcast_select_fusion.1 = (f16[32,16,512]{2,1,0:T(8,128)(2,1)S(1)}, f16[32,16,512]{2,1,0:T(8,128)(2,1)S(1)}) fusion(pred[32]{0:T(512)(128)(4,1)S(1)} %fusion.15, f16[32,16,1024]{2,1,0:T(8,128)(2,1)} %all-to-all-done.2), kind=kLoop, calls=%fused_computation.23 | loop fusion | flops 524288 | bytes 2097184 | tf_op jit(solution)/shard_map/jit(_where)/select_n | solution.py:286
  88.2 0.3 convert_multiply_fusion.rec
  88.5 5.0 %shard_map.112 = (f32[16,16,2048]{2,1,0:T(8,128)}, f32[16,16,2048]{2,1,0:T(8,128)}, bf16[32,16,1536]{2,1,0:T(8,128)(2,1)}) custom-call(s32[32]{0:T(128)S(1)} %select_reduce_fusion.slots, s32[2]{0:T(128)S(1)} %pad_add_fusion.blocks, f32[16]{0:T(128)S(1)} %broadcast_divide_fusion.shares, ...), custom_call_target="tpu_custom_call", output_to_operand_aliasing={{0}: (6, {}), {1}: (7, {})} | custom-call | flops 2097152 | bytes 7340032 | tf_op jit(solution)/shard_map/pallas_call | solution.py:54
  93.5 4.8 %all-to-all-done.3 = f16[32,16,512]{2,1,0:T(8,128)(2,1)} async-done(((f16[32,16,512]{2,1,0:T(8,128)(2,1)}), f16[32,16,512]{2,1,0:T(8,128)(2,1)}, u32[]{:S(2)}, u32[]{:S(2)}) %all-to-all-start.3) | async-done | bytes 524320 | tf_op jit(solution)/shard_map/all_to_all | solution.py:253
  98.3 1.2 convert_multiply_fusion.1.rec
  99.5 2.0 %shard_map.113 = (f32[16,16,2048]{2,1,0:T(8,128)}, f32[16,16,2048]{2,1,0:T(8,128)}, bf16[32,16,1536]{2,1,0:T(8,128)(2,1)}) custom-call(s32[32]{0:T(128)S(1)} %select_reduce_fusion.slots, s32[1]{0:T(128)} %bitcast.1.blocks, f32[16]{0:T(128)S(1)} %broadcast_divide_fusion.shares, ...), custom_call_target="tpu_custom_call", output_to_operand_aliasing={{0}: (6, {}), {1}: (7, {}), {2}: (8, {})} | custom-call | flops 1048576 | bytes 2097152 | tf_op jit(solution)/shard_map/pallas_call | solution.py:117
  101.5 4.7 %all-to-all-start.4 = ((bf16[32,16,1536]{2,1,0:T(8,128)(2,1)}), bf16[32,16,1536]{2,1,0:T(8,128)(2,1)}, u32[]{:S(2)}, u32[]{:S(2)}) async-start(bf16[32,16,1536]{2,1,0:T(8,128)(2,1)} %get-tuple-element.42), calls=%async_computation.4 | async-start | bytes 3145728 | tf_op jit(solution)/shard_map/all_to_all | solution.py:253
  106.3 3.9 %copy.20 = bf16[1,512,2048]{1,2,0:T(8,128)(2,1)} copy(bf16[1,512,2048]{2,1,0:T(8,128)(2,1)} %param.10) | data formatting | bytes 4194304 | tf_op args[2]
  110.2 0.1 add_multiply_fusion.starts
  110.3 0.0 copy-start.1
  110.3 1.6 %copy-done.1 = bf16[2048,512]{1,0:T(8,128)(2,1)S(1)} copy-done((bf16[2048,512]{1,0:T(8,128)(2,1)S(1)}, bf16[2048,512]{1,0:T(8,128)(2,1)}, u32[]{:S(2)}) %copy-start.1) | copy-done | bytes 2097176
  111.9 0.0 copy-start.2
  111.9 1.6 %copy-done.2 = bf16[1,512,2048]{1,2,0:T(8,128)(2,1)S(1)} copy-done((bf16[1,512,2048]{1,2,0:T(8,128)(2,1)S(1)}, bf16[1,512,2048]{1,2,0:T(8,128)(2,1)}, u32[]{:S(2)}) %copy-start.2) | copy-done | bytes 2097176
  113.5 8.1 %shard_map.114 = bf16[2048,512]{1,0:T(8,128)(2,1)} custom-call(s32[4]{0:T(128)S(1)} %add_multiply_fusion.starts, bf16[2048,512]{1,0:T(8,128)(2,1)S(1)} %bitcast.62, bf16[2048,512]{1,0:T(8,128)(2,1)S(1)} %copy-done.1, bf16[2048,512]{1,0:T(8,128)(2,1)} %collective-permute-done.refs_1_, bf16[2048,512]{1,0:T(8,128)(2,1)} %collective-permute-done.1.refs_2_, ...), custom_call_target="tpu_custom_call" | custom-call | flops 4294967296 | bytes 12582912 | tf_op jit(solution)/shard_map/pallas_call | solution.py:187
  121.6 8.6 %all-to-all-done.4 = bf16[32,16,1536]{2,1,0:T(8,128)(2,1)} async-done(((bf16[32,16,1536]{2,1,0:T(8,128)(2,1)}), bf16[32,16,1536]{2,1,0:T(8,128)(2,1)}, u32[]{:S(2)}, u32[]{:S(2)}) %all-to-all-start.4) | async-done | bytes 1572896 | tf_op jit(solution)/shard_map/all_to_all | solution.py:253
  130.2 2.6 %shard_map.115 = bf16[512,2048]{1,0:T(8,128)(2,1)} custom-call(s32[1]{0:T(128)} %bitcast.2.blocks.which, bf16[512,512]{1,0:T(8,128)(2,1)} %bitcast.6.refs_0_, bf16[512,1536]{1,0:T(8,128)(2,1)} %bitcast.18.refs_1_), custom_call_target="tpu_custom_call" | custom-call | bytes 4194304 | tf_op jit(solution)/shard_map/pallas_call | solution.py:155
  (2 shorter events, 0.0 us)
Async XLA Ops:
  0.6 1.7 %copy-start = (bf16[2048,512]{1,0:T(8,128)(2,1)S(1)}, bf16[2048,512]{1,0:T(8,128)(2,1)}, u32[]{:S(2)}) copy-start(bf16[2048,512]{1,0:T(8,128)(2,1)} %param.8) | copy-start | bytes 6291460
  0.6 45.8 %collective-permute-start = (bf16[2048,512]{1,0:T(8,128)(2,1)}, bf16[2048,512]{1,0:T(8,128)(2,1)}, u32[]{:S(2)}, u32[]{:S(2)}) collective-permute-start(bf16[2048,512]{1,0:T(8,128)(2,1)} %refs_0_.1), channel_id=1, source_target_pairs={{0,1},{1,2},{2,3},{3,0},{4,7},{5,4},{6,5},{7,6},{8,9},{9,10},{10,1... | collective-permute-start | bytes 6291464 | tf_op jit(solution)/shard_map/ppermute | solution.py:223
  2.4 15.2 %copy-start.3 = (s32[16]{0:T(128)S(1)}, s32[16]{0:T(128)}, u32[]{:S(2)}) copy-start(s32[16]{0:T(128)} %param.13) | copy-start | bytes 196
  2.4 15.2 %copy-start.4 = (s32[32,1]{0,1:T(1,128)S(1)}, s32[32,1]{0,1:T(1,128)}, u32[]{:S(2)}) copy-start(s32[32,1]{0,1:T(1,128)} %param.12) | copy-start | bytes 388
  6.4 20.5 %all-to-all-start = ((f16[32,16,512]{2,1,0:T(8,128)(2,1)}), f16[32,16,512]{2,1,0:T(8,128)(2,1)S(1)}, u32[]{:S(2)}, u32[]{:S(2)}) async-start(f16[32,16,512]{2,1,0:T(8,128)(2,1)} %bitcast.5), calls=%async_computation | async-start | bytes 1048576 | tf_op jit(solution)/shard_map/all_to_all | solution.py:253
  15.1 38.4 %collective-permute-start.1 = (bf16[2048,512]{1,0:T(8,128)(2,1)}, bf16[2048,512]{1,0:T(8,128)(2,1)}, u32[]{:S(2)}, u32[]{:S(2)}) collective-permute-start(bf16[2048,512]{1,0:T(8,128)(2,1)} %refs_0_.1), channel_id=1, source_target_pairs={{0,3},{1,0},{2,1},{3,2},{4,5},{5,6},{6,7},{7,4},{8,11},{9,8},{10,9... | collective-permute-start | bytes 6291464 | tf_op jit(solution)/shard_map/ppermute | solution.py:223
  30.0 16.4 %all-to-all-start.1 = ((bf16[32,16,512]{2,1,0:T(8,128)(2,1)}), bf16[32,16,512]{2,1,0:T(8,128)(2,1)}, u32[]{:S(2)}, u32[]{:S(2)}) async-start(bf16[32,16,512]{2,1,0:T(8,128)(2,1)} %get-tuple-element.28), calls=%async_computation.1 | async-start | bytes 1048576 | tf_op jit(solution)/shard_map/all_to_all | solution.py:253
  50.4 27.6 %collective-permute-start.2 = (bf16[2048,512]{1,0:T(8,128)(2,1)}, bf16[2048,512]{1,0:T(8,128)(2,1)}, u32[]{:S(2)}, u32[]{:S(2)}) collective-permute-start(bf16[2048,512]{1,0:T(8,128)(2,1)} %collective-permute-done.refs_1_), channel_id=1, source_target_pairs={{0,1},{1,2},{2,3},{3,0},{4,7},{5,4},{6,5},{7,6},{8,9},{9,10},{10,1... | collective-permute-start | bytes 6291464 | tf_op jit(solution)/shard_map/ppermute | solution.py:223
  57.7 24.3 %all-to-all-start.2 = ((f16[32,16,1024]{2,1,0:T(8,128)(2,1)}), f16[32,16,1024]{2,1,0:T(8,128)(2,1)}, u32[]{:S(2)}, u32[]{:S(2)}) async-start(f16[32,16,1024]{2,1,0:T(8,128)(2,1)} %constant_dynamic-update-slice_fusion), calls=%async_computation.2 | async-start | bytes 2097152 | tf_op jit(solution)/shard_map/all_to_all | solution.py:253
  81.9 16.4 %all-to-all-start.3 = ((f16[32,16,512]{2,1,0:T(8,128)(2,1)}), f16[32,16,512]{2,1,0:T(8,128)(2,1)}, u32[]{:S(2)}, u32[]{:S(2)}) async-start(f16[32,16,512]{2,1,0:T(8,128)(2,1)} %bitcast.64), calls=%async_computation.3 | async-start | bytes 1048576 | tf_op jit(solution)/shard_map/all_to_all | solution.py:253
  101.5 28.6 %all-to-all-start.4 = ((bf16[32,16,1536]{2,1,0:T(8,128)(2,1)}), bf16[32,16,1536]{2,1,0:T(8,128)(2,1)}, u32[]{:S(2)}, u32[]{:S(2)}) async-start(bf16[32,16,1536]{2,1,0:T(8,128)(2,1)} %get-tuple-element.42), calls=%async_computation.4 | async-start | bytes 3145728 | tf_op jit(solution)/shard_map/all_to_all | solution.py:253
  110.3 1.6 %copy-start.1 = (bf16[2048,512]{1,0:T(8,128)(2,1)S(1)}, bf16[2048,512]{1,0:T(8,128)(2,1)}, u32[]{:S(2)}) copy-start(bf16[2048,512]{1,0:T(8,128)(2,1)} %refs_0_.1) | copy-start | bytes 6291460
  111.9 1.6 %copy-start.2 = (bf16[1,512,2048]{1,2,0:T(8,128)(2,1)S(1)}, bf16[1,512,2048]{1,2,0:T(8,128)(2,1)}, u32[]{:S(2)}) copy-start(bf16[1,512,2048]{1,2,0:T(8,128)(2,1)} %copy.20) | copy-start | bytes 6291460

commit v6 on v4

--- a/solution.py
+++ b/solution.py
@@ -151,7 +151,6 @@
 def place(orders, which, pieces):
     rows, width = pieces[0].shape
     whole = len(orders[0]) * width
-    pieces = [pltpu.with_memory_space_constraint(piece, pltpu.HBM) for piece in pieces]
     tile = rows // 2
     return pl.pallas_call(
         functools.partial(place_kernel, orders),

time: 134 us -> 134 us (level)
  no operation moved by 1% of the time
where the time goes in v6:
time: 134 us; the launch traced here: 133 us
  waiting for transfers between devices  47.2 us (35%)
  starting transfers between devices  35.7 us (27%)
  Pallas kernels  20.7 us (15%)
  matrix products  15.2 us (11%)
  local copies, waits for them, and re-layouts  8.41 us (6%)
  other arithmetic  4.76 us (4%)
    all_to_all x5, waiting for transfers between devices, exchange(): lax.all_to_all(pieces, 'path', split_axis=0, concat_axis=0, tiled=True)  33 us
    all_to_all x5, starting transfers between devices, exchange(): lax.all_to_all(pieces, 'path', split_axis=0, concat_axis=0, tiled=True)  30.6 us
    dot_general x4, matrix products, pseudo_pieces(): raw = jnp.dot(turned_inputs, block, preferred_element_type=jnp.float32)  15.2 us
    ppermute x3, waiting for transfers between devices, stepped(): lax.ppermute(block, ('path', 'shard'), [(p * size + y, p * size + (y + (s...  14.2 us
    pallas_call x1, Pallas kernels, input_gradient(): pl.pallas_call(functools.partial(back_kernel, scale), grid_spec=pltpu.Pre...  8.1 us
    pallas_call x2, Pallas kernels, update(): pl.pallas_call(functools.partial(update_kernel, stores, out_width > 0), g...  7.96 us
    unnamed x13, local copies, waits for them, and re-layouts  7.13 us
    ppermute x3, starting transfers between devices, stepped(): lax.ppermute(block, ('path', 'shard'), [(p * size + y, p * size + (y + (s...  5.13 us
  transfers between devices with their start and end apart: 8, of which 5 were waited for; matrix products, arithmetic and copies ran while one was open for 18% of the time, Pallas kernels for 12%

profile of v6, /device:TPU:0, one launch (start us, length us, event | category | flops | bytes accessed | tf_op | source)
XLA Modules:
  0.0 132.8 jit_solution(6513094160057843596)
XLA Ops:
  0.6 0.0 copy-start
  0.6 1.7 %collective-permute-start = (bf16[2048,512]{1,0:T(8,128)(2,1)}, bf16[2048,512]{1,0:T(8,128)(2,1)}, u32[]{:S(2)}, u32[]{:S(2)}) collective-permute-start(bf16[2048,512]{1,0:T(8,128)(2,1)} %refs_0_.1), channel_id=1, source_target_pairs={{0,1},{1,2},{2,3},{3,0},{4,7},{5,4},{6,5},{7,6},{8,9},{9,10},{10,1... | collective-permute-start | bytes 6291464 | tf_op jit(solution)/shard_map/ppermute | solution.py:223
  2.4 0.0 copy-done
  2.4 0.0 copy-start.4
  2.4 0.0 copy-start.5
  2.4 4.0 %fusion.14 = f16[512,512]{1,0:T(8,128)(2,1)} fusion(bf16[512,2048]{0,1:T(8,128)(2,1)S(1)} %bitcast.59, bf16[2048,512]{1,0:T(8,128)(2,1)} %refs_0_.1, f32[1,512,2048]{2,1,0:T(8,128)} %param.11, s32[]{:T(128)S(6)} %select_n.64), kind=kOutput, calls=%fused_computation.19 | convolution fusion | flops 1074790400 | bytes 5767172 | tf_op jit(solution)/shard_map/dot_general | solution.py:248
  6.4 8.8 %all-to-all-start = ((f16[32,16,512]{2,1,0:T(8,128)(2,1)}), f16[32,16,512]{2,1,0:T(8,128)(2,1)S(1)}, u32[]{:S(2)}, u32[]{:S(2)}) async-start(f16[32,16,512]{2,1,0:T(8,128)(2,1)} %bitcast.5), calls=%async_computation | async-start | bytes 1048576 | tf_op jit(solution)/shard_map/all_to_all | solution.py:253
  15.1 2.4 %collective-permute-start.1 = (bf16[2048,512]{1,0:T(8,128)(2,1)}, bf16[2048,512]{1,0:T(8,128)(2,1)}, u32[]{:S(2)}, u32[]{:S(2)}) collective-permute-start(bf16[2048,512]{1,0:T(8,128)(2,1)} %refs_0_.1), channel_id=1, source_target_pairs={{0,3},{1,0},{2,1},{3,2},{4,5},{5,6},{6,7},{7,4},{8,11},{9,8},{10,9... | collective-permute-start | bytes 6291464 | tf_op jit(solution)/shard_map/ppermute | solution.py:223
  17.5 0.0 copy-done.4
  17.6 0.0 copy-done.5
  17.6 0.1 select_reduce_fusion.slots
  17.6 0.1 convert_reduce_fusion
  17.8 9.1 %all-to-all-done = f16[32,16,512]{2,1,0:T(8,128)(2,1)S(1)} async-done(((f16[32,16,512]{2,1,0:T(8,128)(2,1)}), f16[32,16,512]{2,1,0:T(8,128)(2,1)S(1)}, u32[]{:S(2)}, u32[]{:S(2)}) %all-to-all-start) | async-done | bytes 524320 | tf_op jit(solution)/shard_map/all_to_all | solution.py:253
  26.9 0.1 convert_multiply_fusion.2.rec
  27.0 3.0 %shard_map.111 = (f32[16,16,2048]{2,1,0:T(8,128)}, f32[16,16,2048]{2,1,0:T(8,128)}, bf16[32,16,512]{2,1,0:T(8,128)(2,1)}) custom-call(s32[32]{0:T(128)S(1)} %select_reduce_fusion.slots, s32[1]{0:T(128)} %bitcast.2.blocks.which, f32[16]{0:T(128)S(1)} %broadcast_divide_fusion.shares, f32[32,16,512]{2,1,0:T(8,128)S(1)} %convert_multiply_fusion.2.rec, ...), custom_call_target="tpu_custom_call" | custom-call | flops 1048576 | bytes 3670016 | tf_op jit(solution)/shard_map/pallas_call | solution.py:54
  30.0 4.6 %all-to-all-start.1 = ((bf16[32,16,512]{2,1,0:T(8,128)(2,1)}), bf16[32,16,512]{2,1,0:T(8,128)(2,1)}, u32[]{:S(2)}, u32[]{:S(2)}) async-start(bf16[32,16,512]{2,1,0:T(8,128)(2,1)} %get-tuple-element.28), calls=%async_computation.1 | async-start | bytes 1048576 | tf_op jit(solution)/shard_map/all_to_all | solution.py:253
  34.7 1.3 constant_dynamic-slice_fusion
  36.0 10.4 %all-to-all-done.1 = bf16[32,16,512]{2,1,0:T(8,128)(2,1)} async-done(((bf16[32,16,512]{2,1,0:T(8,128)(2,1)}), bf16[32,16,512]{2,1,0:T(8,128)(2,1)}, u32[]{:S(2)}, u32[]{:S(2)}) %all-to-all-start.1) | async-done | bytes 524320 | tf_op jit(solution)/shard_map/all_to_all | solution.py:253
  46.4 0.0 collective-permute-done.refs_1_
  46.4 4.0 %fusion.13 = f16[512,512]{1,0:T(8,128)(2,1)} fusion(bf16[2048,512]{1,0:T(8,128)(2,1)} %collective-permute-done.refs_1_, bf16[512,2048]{0,1:T(8,128)(2,1)S(1)} %bitcast.60, f32[1,512,2048]{2,1,0:T(8,128)} %param.11, s32[]{:T(128)S(6)} %select_n.70), kind=kOutput, calls=%fused_computation.18 | convolution fusion | flops 1074790400 | bytes 5767172 | tf_op jit(solution)/shard_map/dot_general | solution.py:248
  50.4 1.0 collective-permute-start.2
  51.4 0.0 copy-start.3
  51.4 0.0 collective-permute-done.1.refs_2_
  51.4 3.2 %fusion.12 = f16[512,512]{1,0:T(8,128)(2,1)S(1)} fusion(bf16[2048,512]{1,0:T(8,128)(2,1)} %collective-permute-done.1.refs_2_, bf16[512,2048]{0,1:T(8,128)(2,1)S(1)} %bitcast.61, f32[1,512,2048]{2,1,0:T(8,128)} %param.11, s32[]{:T(128)S(6)} %select_n.72), kind=kOutput, calls=%fused_computation.17 | convolution fusion | flops 1074790400 | bytes 5767172 | tf_op jit(solution)/shard_map/dot_general | solution.py:248
  54.6 0.0 copy-done.3
  54.6 1.2 pad_maximum_fusion
  55.9 7.9 %all-to-all-start.2 = ((f16[32,16,1024]{2,1,0:T(8,128)(2,1)}), f16[32,16,1024]{2,1,0:T(8,128)(2,1)}, u32[]{:S(2)}, u32[]{:S(2)}) async-start(f16[32,16,1024]{2,1,0:T(8,128)(2,1)} %pad_maximum_fusion), calls=%async_computation.2 | async-start | bytes 2097152 | tf_op jit(solution)/shard_map/all_to_all | solution.py:253
  63.7 14.2 %collective-permute-done.2.refs_3_ = bf16[2048,512]{1,0:T(8,128)(2,1)} collective-permute-done((bf16[2048,512]{1,0:T(8,128)(2,1)}, bf16[2048,512]{1,0:T(8,128)(2,1)}, u32[]{:S(2)}, u32[]{:S(2)}) %collective-permute-start.2) | collective-permute-done | bytes 2097184 | tf_op jit(solution)/shard_map/ppermute | solution.py:223
  77.9 4.0 %fusion.11 = f16[512,512]{1,0:T(8,128)(2,1)} fusion(bf16[2048,512]{1,0:T(8,128)(2,1)} %collective-permute-done.2.refs_3_, bf16[512,2048]{0,1:T(8,128)(2,1)S(1)} %bitcast.58, f32[1,512,2048]{2,1,0:T(8,128)} %param.11, s32[]{:T(128)S(6)} %select_n.65), kind=kOutput, calls=%fused_computation.16 | convolution fusion | flops 1074790400 | bytes 5767172 | tf_op jit(solution)/shard_map/dot_general | solution.py:248
  81.9 0.0 all-to-all-done.2
  81.9 4.6 %all-to-all-start.3 = ((f16[32,16,512]{2,1,0:T(8,128)(2,1)}), f16[32,16,512]{2,1,0:T(8,128)(2,1)}, u32[]{:S(2)}, u32[]{:S(2)}) async-start(f16[32,16,512]{2,1,0:T(8,128)(2,1)} %bitcast.64), calls=%async_computation.3 | async-start | bytes 1048576 | tf_op jit(solution)/shard_map/all_to_all | solution.py:253
  86.5 0.1 pad_add_fusion.blocks
  86.6 1.5 %broadcast_select_fusion.1 = (f16[32,16,512]{2,1,0:T(8,128)(2,1)S(1)}, f16[32,16,512]{2,1,0:T(8,128)(2,1)S(1)}) fusion(pred[32]{0:T(512)(128)(4,1)S(1)} %fusion.15, f16[32,16,1024]{2,1,0:T(8,128)(2,1)} %all-to-all-done.2), kind=kLoop, calls=%fused_computation.24 | loop fusion | flops 524288 | bytes 2097184 | tf_op jit(solution)/shard_map/jit(_where)/select_n | solution.py:285
  88.2 0.3 convert_multiply_fusion.rec
  88.5 5.0 %shard_map.112 = (f32[16,16,2048]{2,1,0:T(8,128)}, f32[16,16,2048]{2,1,0:T(8,128)}, bf16[32,16,1536]{2,1,0:T(8,128)(2,1)}) custom-call(s32[32]{0:T(128)S(1)} %select_reduce_fusion.slots, s32[2]{0:T(128)S(1)} %pad_add_fusion.blocks, f32[16]{0:T(128)S(1)} %broadcast_divide_fusion.shares, ...), custom_call_target="tpu_custom_call", output_to_operand_aliasing={{0}: (6, {}), {1}: (7, {})} | custom-call | flops 2097152 | bytes 7340032 | tf_op jit(solution)/shard_map/pallas_call | solution.py:54
  93.4 4.8 %all-to-all-done.3 = f16[32,16,512]{2,1,0:T(8,128)(2,1)} async-done(((f16[32,16,512]{2,1,0:T(8,128)(2,1)}), f16[32,16,512]{2,1,0:T(8,128)(2,1)}, u32[]{:S(2)}, u32[]{:S(2)}) %all-to-all-start.3) | async-done | bytes 524320 | tf_op jit(solution)/shard_map/all_to_all | solution.py:253
  98.3 1.2 convert_multiply_fusion.1.rec
  99.5 2.0 %shard_map.113 = (f32[16,16,2048]{2,1,0:T(8,128)}, f32[16,16,2048]{2,1,0:T(8,128)}, bf16[32,16,1536]{2,1,0:T(8,128)(2,1)}) custom-call(s32[32]{0:T(128)S(1)} %select_reduce_fusion.slots, s32[1]{0:T(128)} %bitcast.1.blocks, f32[16]{0:T(128)S(1)} %broadcast_divide_fusion.shares, ...), custom_call_target="tpu_custom_call", output_to_operand_aliasing={{0}: (6, {}), {1}: (7, {}), {2}: (8, {})} | custom-call | flops 1048576 | bytes 2097152 | tf_op jit(solution)/shard_map/pallas_call | solution.py:117
  101.5 4.7 %all-to-all-start.4 = ((bf16[32,16,1536]{2,1,0:T(8,128)(2,1)}), bf16[32,16,1536]{2,1,0:T(8,128)(2,1)}, u32[]{:S(2)}, u32[]{:S(2)}) async-start(bf16[32,16,1536]{2,1,0:T(8,128)(2,1)} %get-tuple-element.42), calls=%async_computation.4 | async-start | bytes 3145728 | tf_op jit(solution)/shard_map/all_to_all | solution.py:253
  106.3 3.9 %copy.20 = bf16[1,512,2048]{1,2,0:T(8,128)(2,1)} copy(bf16[1,512,2048]{2,1,0:T(8,128)(2,1)} %param.10) | data formatting | bytes 4194304 | tf_op args[2]
  110.2 0.1 add_multiply_fusion.starts
  110.3 0.0 copy-start.1
  110.3 1.6 %copy-done.1 = bf16[2048,512]{1,0:T(8,128)(2,1)S(1)} copy-done((bf16[2048,512]{1,0:T(8,128)(2,1)S(1)}, bf16[2048,512]{1,0:T(8,128)(2,1)}, u32[]{:S(2)}) %copy-start.1) | copy-done | bytes 2097176
  111.8 0.0 copy-start.2
  111.9 1.6 %copy-done.2 = bf16[1,512,2048]{1,2,0:T(8,128)(2,1)S(1)} copy-done((bf16[1,512,2048]{1,2,0:T(8,128)(2,1)S(1)}, bf16[1,512,2048]{1,2,0:T(8,128)(2,1)}, u32[]{:S(2)}) %copy-start.2) | copy-done | bytes 2097176
  113.4 8.1 %shard_map.114 = bf16[2048,512]{1,0:T(8,128)(2,1)} custom-call(s32[4]{0:T(128)S(1)} %add_multiply_fusion.starts, bf16[2048,512]{1,0:T(8,128)(2,1)S(1)} %bitcast.62, bf16[2048,512]{1,0:T(8,128)(2,1)S(1)} %copy-done.1, bf16[2048,512]{1,0:T(8,128)(2,1)} %collective-permute-done.refs_1_, bf16[2048,512]{1,0:T(8,128)(2,1)} %collective-permute-done.1.refs_2_, ...), custom_call_target="tpu_custom_call" | custom-call | flops 4294967296 | bytes 12582912 | tf_op jit(solution)/shard_map/pallas_call | solution.py:187
  121.5 8.6 %all-to-all-done.4 = bf16[32,16,1536]{2,1,0:T(8,128)(2,1)} async-done(((bf16[32,16,1536]{2,1,0:T(8,128)(2,1)}), bf16[32,16,1536]{2,1,0:T(8,128)(2,1)}, u32[]{:S(2)}, u32[]{:S(2)}) %all-to-all-start.4) | async-done | bytes 1572896 | tf_op jit(solution)/shard_map/all_to_all | solution.py:253
  130.2 2.6 %shard_map.115 = bf16[512,2048]{1,0:T(8,128)(2,1)} custom-call(s32[1]{0:T(128)} %bitcast.2.blocks.which, bf16[512,512]{1,0:T(8,128)(2,1)} %bitcast.6.refs_0_, bf16[512,1536]{1,0:T(8,128)(2,1)} %bitcast.18.refs_1_), custom_call_target="tpu_custom_call" | custom-call | bytes 4194304 | tf_op jit(solution)/shard_map/pallas_call | solution.py:155
  (2 shorter events, 0.0 us)
Async XLA Ops:
  0.6 1.7 %copy-start = (bf16[2048,512]{1,0:T(8,128)(2,1)S(1)}, bf16[2048,512]{1,0:T(8,128)(2,1)}, u32[]{:S(2)}) copy-start(bf16[2048,512]{1,0:T(8,128)(2,1)} %param.8) | copy-start | bytes 6291460
  0.6 45.8 %collective-permute-start = (bf16[2048,512]{1,0:T(8,128)(2,1)}, bf16[2048,512]{1,0:T(8,128)(2,1)}, u32[]{:S(2)}, u32[]{:S(2)}) collective-permute-start(bf16[2048,512]{1,0:T(8,128)(2,1)} %refs_0_.1), channel_id=1, source_target_pairs={{0,1},{1,2},{2,3},{3,0},{4,7},{5,4},{6,5},{7,6},{8,9},{9,10},{10,1... | collective-permute-start | bytes 6291464 | tf_op jit(solution)/shard_map/ppermute | solution.py:223
  2.4 15.2 %copy-start.4 = (s32[16]{0:T(128)S(1)}, s32[16]{0:T(128)}, u32[]{:S(2)}) copy-start(s32[16]{0:T(128)} %param.13) | copy-start | bytes 196
  2.4 15.2 %copy-start.5 = (s32[32,1]{0,1:T(1,128)S(1)}, s32[32,1]{0,1:T(1,128)}, u32[]{:S(2)}) copy-start(s32[32,1]{0,1:T(1,128)} %param.12) | copy-start | bytes 388
  6.4 20.5 %all-to-all-start = ((f16[32,16,512]{2,1,0:T(8,128)(2,1)}), f16[32,16,512]{2,1,0:T(8,128)(2,1)S(1)}, u32[]{:S(2)}, u32[]{:S(2)}) async-start(f16[32,16,512]{2,1,0:T(8,128)(2,1)} %bitcast.5), calls=%async_computation | async-start | bytes 1048576 | tf_op jit(solution)/shard_map/all_to_all | solution.py:253
  15.1 36.2 %collective-permute-start.1 = (bf16[2048,512]{1,0:T(8,128)(2,1)}, bf16[2048,512]{1,0:T(8,128)(2,1)}, u32[]{:S(2)}, u32[]{:S(2)}) collective-permute-start(bf16[2048,512]{1,0:T(8,128)(2,1)} %refs_0_.1), channel_id=1, source_target_pairs={{0,3},{1,0},{2,1},{3,2},{4,5},{5,6},{6,7},{7,4},{8,11},{9,8},{10,9... | collective-permute-start | bytes 6291464 | tf_op jit(solution)/shard_map/ppermute | solution.py:223
  30.0 16.4 %all-to-all-start.1 = ((bf16[32,16,512]{2,1,0:T(8,128)(2,1)}), bf16[32,16,512]{2,1,0:T(8,128)(2,1)}, u32[]{:S(2)}, u32[]{:S(2)}) async-start(bf16[32,16,512]{2,1,0:T(8,128)(2,1)} %get-tuple-element.28), calls=%async_computation.1 | async-start | bytes 1048576 | tf_op jit(solution)/shard_map/all_to_all | solution.py:253
  50.4 27.6 %collective-permute-start.2 = (bf16[2048,512]{1,0:T(8,128)(2,1)}, bf16[2048,512]{1,0:T(8,128)(2,1)}, u32[]{:S(2)}, u32[]{:S(2)}) collective-permute-start(bf16[2048,512]{1,0:T(8,128)(2,1)} %collective-permute-done.refs_1_), channel_id=1, source_target_pairs={{0,1},{1,2},{2,3},{3,0},{4,7},{5,4},{6,5},{7,6},{8,9},{9,10},{10,1... | collective-permute-start | bytes 6291464 | tf_op jit(solution)/shard_map/ppermute | solution.py:223
  51.4 3.3 %copy-start.3 = (f16[512,512]{1,0:T(8,128)(2,1)S(1)}, f16[512,512]{1,0:T(8,128)(2,1)}, u32[]{:S(2)}) copy-start(f16[512,512]{1,0:T(8,128)(2,1)} %fusion.13) | copy-start | bytes 1572868
  55.9 26.1 %all-to-all-start.2 = ((f16[32,16,1024]{2,1,0:T(8,128)(2,1)}), f16[32,16,1024]{2,1,0:T(8,128)(2,1)}, u32[]{:S(2)}, u32[]{:S(2)}) async-start(f16[32,16,1024]{2,1,0:T(8,128)(2,1)} %pad_maximum_fusion), calls=%async_computation.2 | async-start | bytes 2097152 | tf_op jit(solution)/shard_map/all_to_all | solution.py:253
  81.9 16.4 %all-to-all-start.3 = ((f16[32,16,512]{2,1,0:T(8,128)(2,1)}), f16[32,16,512]{2,1,0:T(8,128)(2,1)}, u32[]{:S(2)}, u32[]{:S(2)}) async-start(f16[32,16,512]{2,1,0:T(8,128)(2,1)} %bitcast.64), calls=%async_computation.3 | async-start | bytes 1048576 | tf_op jit(solution)/shard_map/all_to_all | solution.py:253
  101.5 28.6 %all-to-all-start.4 = ((bf16[32,16,1536]{2,1,0:T(8,128)(2,1)}), bf16[32,16,1536]{2,1,0:T(8,128)(2,1)}, u32[]{:S(2)}, u32[]{:S(2)}) async-start(bf16[32,16,1536]{2,1,0:T(8,128)(2,1)} %get-tuple-element.42), calls=%async_computation.4 | async-start | bytes 3145728 | tf_op jit(solution)/shard_map/all_to_all | solution.py:253
  110.3 1.6 %copy-start.1 = (bf16[2048,512]{1,0:T(8,128)(2,1)S(1)}, bf16[2048,512]{1,0:T(8,128)(2,1)}, u32[]{:S(2)}) copy-start(bf16[2048,512]{1,0:T(8,128)(2,1)} %refs_0_.1) | copy-start | bytes 6291460
  111.8 1.6 %copy-start.2 = (bf16[1,512,2048]{1,2,0:T(8,128)(2,1)S(1)}, bf16[1,512,2048]{1,2,0:T(8,128)(2,1)}, u32[]{:S(2)}) copy-start(bf16[1,512,2048]{1,2,0:T(8,128)(2,1)} %copy.20) | copy-start | bytes 6291460
